TPU v7x, 32 devices: a whole 2x2x4 slice. The times are simulated.
32 devices in a mesh: rep: 8 (over z, x), layer: 4 (over y, core).
Axes of the slice: x: 2, y: 2, z: 4, core: 2. Of those that a mesh axis runs over, the one named last changes fastest.
Arguments:
- activations: bfloat16 [4, 4096, 8192], P('layer', 'rep'), may hold values from -6 to 6
- output_grads: bfloat16 [4, 4096, 8192], P('layer', 'rep'), may hold values from -6 to 6
- in_projection: bfloat16 [4, 32, 8192], P('layer'), may hold values from -0.0625 to 0.0625
- out_projection: bfloat16 [4, 32, 8192], P('layer'), may hold values from -0.0625 to 0.0625
- segment_ids: int32 [4096], P('rep'), may hold values from -1 to 61, as said below
- move_list: int32 [496], P('rep'), may hold values from -1 to 255, as said below
Outputs:
- factor: float32 [4, 1024, 1024], P('layer')
- features: bfloat16 [4, 256, 1024], P('layer', 'rep')
- self_influence: float32 [256], P('rep')
Inputs may be any that keep to these rules, and one draw needn't show every extreme that they name: `segment_ids`: within each replica's 512 tokens the values never fall; a run of equal values is one document; -1 marks tokens continuing the previous replica's last document and never occurs on replica 0; n documents start on a replica with values 0 to n - 1, n from 2 to 62, and some replica has exactly 62; all documents together are 256; the last document ends at the end of the last replica. `move_list`: replica r's block of 62 entries gives for its documents in order of their first token (the one continuing onto replica r + 1 included) the destination row in 0 to 255, and -1 past its last document; every row is named exactly once; the documents of replica r go to rows of replica r - 1, r or r + 1 (rows m * 32 to m * 32 + 31 belong to replica m).
All inputs are finite; a program needn't handle non-finite values.
Results may differ from a plain program's by a relative error of at most 0.0064.
Values may be sent and summed in bfloat16 or wider, within the bound.
No kernel may reach another device: no remote copies, remote signals or barrier semaphores. Data moves between devices by JAX's collectives and lax.ppermute only.
A program may use at most 128 MiB of HBM per device.

v0:
```python
import jax
import jax.numpy as jnp
from jax import lax
from jax.sharding import PartitionSpec as P

BAL = 32


DAMPING = 0.05


def shifted(block, axis, distance):
    devices = range(lax.axis_size(axis))
    route = [(i - distance, i) for i in devices if i - distance in devices]
    return lax.ppermute(block, axis, route)


def on_device(activations, output_grads, in_projection, out_projection, segment_ids, move_list):
    contract = (((1,), (1,)), ((), ()))
    left = lax.dot_general(
        in_projection[0], activations[0], contract, preferred_element_type=jnp.float32
    ).astype(jnp.bfloat16)
    right = lax.dot_general(
        out_projection[0], output_grads[0], contract, preferred_element_type=jnp.float32
    ).astype(jnp.bfloat16)
    doc_slots = move_list.shape[0]
    width = left.shape[0] * right.shape[0]
    slot_ids = jnp.arange(doc_slots + 1, dtype=jnp.int32) - 1
    member = (segment_ids[None, :] == slot_ids[:, None]).astype(jnp.bfloat16)
    masked = member[:, None, :] * left[None, :, :]
    blocks = lax.dot_general(
        masked, right, (((2,), (1,)), ((), ())), preferred_element_type=jnp.float32
    )
    sums = blocks.reshape(doc_slots + 1, width)
    counts = jnp.sum(member.astype(jnp.float32), axis=1)
    carried_sum, carried_count = shifted((sums[:1], counts[:1]), "rep", -1)
    last_slot = jnp.max(segment_ids)
    takes = (slot_ids[1:] == last_slot).astype(jnp.float32)
    totals = sums[1:] + takes[:, None] * carried_sum
    lengths = counts[1:] + takes * carried_count[0]
    safe_len = jnp.maximum(lengths, 1.0)
    local_features = (totals / jnp.sqrt(safe_len)[:, None]).astype(jnp.bfloat16)
    replica = lax.axis_index("rep")
    n_rep = lax.axis_size("rep")
    offsets = jnp.where(move_list >= 0, move_list // BAL - replica, 5)
    within = move_list % BAL
    row_ids = jnp.arange(BAL, dtype=jnp.int32)

    def arrange(step_offset):
        select = ((offsets[None, :] == step_offset) & (within[None, :] == row_ids[:, None])).astype(
            jnp.bfloat16
        )
        return jnp.dot(select, local_features, preferred_element_type=jnp.float32).astype(
            jnp.bfloat16
        )

    staying = arrange(0)
    from_right = shifted(arrange(-1), "rep", -1)
    from_left = shifted(arrange(1), "rep", 1)
    mine = (
        staying.astype(jnp.float32) + from_right.astype(jnp.float32) + from_left.astype(jnp.float32)
    ).astype(jnp.bfloat16)
    rows_contract = (((0,), (0,)), ((), ()))
    local_gram = lax.dot_general(mine, mine, rows_contract, preferred_element_type=jnp.float32)
    gram = lax.psum(local_gram, "rep")
    total_docs = BAL * n_rep
    hessian = gram / total_docs + DAMPING * jnp.eye(width, dtype=jnp.float32)
    lower = jnp.linalg.cholesky(hessian)
    solved = lax.linalg.triangular_solve(
        lower, mine.T.astype(jnp.float32), left_side=True, lower=True
    )
    quad = jnp.sum(solved * solved, axis=0) / width
    influence = lax.psum(quad, "layer")
    return (lower.T[None], mine[None], influence)


def solution(mesh):
    placed = (
        P("layer", "rep", None),
        P("layer", "rep", None),
        P("layer", None, None),
        P("layer", None, None),
        P("rep"),
        P("rep"),
    )
    return jax.shard_map(
        on_device,
        mesh=mesh,
        in_specs=placed,
        out_specs=(P("layer", None, None), P("layer", "rep", None), P("rep")),
        check_vma=False,
    )
```

profile of v0, /device:TPU:0, one launch (start us, length us, event | category | flops | bytes accessed | tf_op | source)
XLA Modules:
  0.0 561.0 jit_solution(721162105258874238)
XLA Ops:
  7.2 0.9 convert_reduce_fusion
  8.1 1.3 collective-permute-start.1
  10.2 6.2 %fusion.10 = bf16[32,512]{1,0:T(8,128)(2,1)S(1)} fusion(bf16[1,512,8192]{2,1,0:T(8,128)(2,1)} %param.6, bf16[1,32,8192]{2,1,0:T(8,128)(2,1)} %param.8), kind=kOutput, calls=%fused_computation.33 | convolution fusion | flops 268451840 | bytes 8945664 | tf_op jit(solution)/shard_map/dot_general | solution.py:20
  16.4 6.7 %fusion.7 = f32[63,32,32]{2,1,0:T(8,128)S(1)} fusion(bf16[32,512]{1,0:T(8,128)(2,1)S(1)} %fusion.10, bf16[63,512]{1,0:T(8,128)(2,1)S(1)} %compare_convert_fusion, bf16[1,512,8192]{2,1,0:T(8,128)(2,1)} %param.7, bf16[1,32,8192]{2,1,0:T(8,128)(2,1)S(1)} %copy-done), kind=kOutput, calls=%fused_computation.14 | convolution fusion | flops 335544320 | bytes 9268224 | tf_op jit(solution)/shard_map/dot_general | solution.py:31
  23.2 1.3 collective-permute-start
  26.7 1.4 maximum_sqrt_fusion
  28.1 2.2 collective-permute-done
  30.6 4.8 collective-permute-start.3
  35.6 1.3 collective-permute-start.2
  37.4 4.5 collective-permute-done.2
  41.9 2.8 fusion.102
  44.7 158.6 %all-reduce.3.cloned.1.call-done = f32[1024,1024]{0,1:T(8,128)} async-done(((f32[1024,1024]{0,1:T(8,128)}), f32[1024,1024]{0,1:T(8,128)}) %all-reduce.3.cloned.1.call-update) | async-done | bytes 4194320 | tf_op jit(solution)/shard_map/psum | solution.py:65
  203.3 5.1 select_add_fusion
  208.4 5.5 copy.29
  213.9 4.5 fusion.4
  218.4 2.0 copy-done.2
  220.4 11.7 %cholesky.222 = f32[128,128]{1,0:T(8,128)S(1)} custom-call(f32[128,128]{1,0:T(8,128)S(1)} %cholesky.577), custom_call_target="Cholesky" | custom-call | tf_op jit(solution)/shard_map/jit(cholesky)/cholesky | solution.py:68
  232.2 9.8 %custom-call.62 = f32[1,128,128]{1,2,0:T(8,128)S(1)} custom-call(f32[1,128,128]{2,1,0:T(8,128)S(1)} %get-tuple-element.48), custom_call_target="InvertDiagBlocksLowerTriangular" | custom-call | tf_op jit(solution)/shard_map/jit(cholesky)/cholesky | solution.py:68
  242.1 1.5 fusion.35
  243.8 1.6 convolution_subtract_fusion
  245.4 11.7 %cholesky.243 = f32[128,128]{1,0:T(8,128)S(1)} custom-call(f32[128,128]{1,0:T(8,128)S(1)} %cholesky.581), custom_call_target="Cholesky" | custom-call | tf_op jit(solution)/shard_map/jit(cholesky)/cholesky | solution.py:68
  257.4 9.8 %custom-call.63 = f32[1,128,128]{1,2,0:T(8,128)S(1)} custom-call(f32[1,128,128]{2,1,0:T(8,128)S(1)} %get-tuple-element.46), custom_call_target="InvertDiagBlocksLowerTriangular" | custom-call | tf_op jit(solution)/shard_map/jit(cholesky)/cholesky | solution.py:68
  268.4 2.0 copy-done.1
  270.3 2.4 convolution_subtract_fusion.1
  272.7 11.7 %cholesky.466 = f32[128,128]{1,0:T(8,128)S(1)} custom-call(f32[128,128]{1,0:T(8,128)S(1)} %cholesky.586), custom_call_target="Cholesky" | custom-call | tf_op jit(solution)/shard_map/jit(cholesky)/cholesky | solution.py:68
  285.2 9.8 %custom-call.64 = f32[1,128,128]{1,2,0:T(8,128)S(1)} custom-call(f32[1,128,128]{2,1,0:T(8,128)S(1)} %get-tuple-element.44), custom_call_target="InvertDiagBlocksLowerTriangular" | custom-call | tf_op jit(solution)/shard_map/jit(cholesky)/cholesky | solution.py:68
  295.0 1.3 convolution_dynamic-update-slice_fusion.1
  296.3 3.5 convolution_subtract_fusion.2
  299.8 11.7 %cholesky.485 = f32[128,128]{1,0:T(8,128)S(1)} custom-call(f32[128,128]{1,0:T(8,128)S(1)} %cholesky.591), custom_call_target="Cholesky" | custom-call | tf_op jit(solution)/shard_map/jit(cholesky)/cholesky | solution.py:68
  312.3 9.8 %custom-call.65 = f32[1,128,128]{1,2,0:T(8,128)S(1)} custom-call(f32[1,128,128]{2,1,0:T(8,128)S(1)} %get-tuple-element.42), custom_call_target="InvertDiagBlocksLowerTriangular" | custom-call | tf_op jit(solution)/shard_map/jit(cholesky)/cholesky | solution.py:68
  322.2 1.1 convolution_dynamic-update-slice_fusion.2
  323.3 3.1 convolution_subtract_fusion.3
  326.5 11.9 %cholesky.504 = f32[128,128]{1,0:T(8,128)S(1)} custom-call(f32[128,128]{1,0:T(8,128)S(1)} %cholesky.596), custom_call_target="Cholesky" | custom-call | tf_op jit(solution)/shard_map/jit(cholesky)/cholesky | solution.py:68
  339.1 9.8 %custom-call.66 = f32[1,128,128]{1,2,0:T(8,128)S(1)} custom-call(f32[1,128,128]{2,1,0:T(8,128)S(1)} %get-tuple-element.40), custom_call_target="InvertDiagBlocksLowerTriangular" | custom-call | tf_op jit(solution)/shard_map/jit(cholesky)/cholesky | solution.py:68
  348.9 1.1 convolution_dynamic-update-slice_fusion.3
  350.0 3.1 convolution_subtract_fusion.4
  353.1 11.7 %cholesky.524 = f32[128,128]{1,0:T(8,128)S(1)} custom-call(f32[128,128]{1,0:T(8,128)S(1)} %cholesky.601), custom_call_target="Cholesky" | custom-call | tf_op jit(solution)/shard_map/jit(cholesky)/cholesky | solution.py:68
  365.6 9.8 %custom-call.67 = f32[1,128,128]{1,2,0:T(8,128)S(1)} custom-call(f32[1,128,128]{2,1,0:T(8,128)S(1)} %get-tuple-element.38), custom_call_target="InvertDiagBlocksLowerTriangular" | custom-call | tf_op jit(solution)/shard_map/jit(cholesky)/cholesky | solution.py:68
  375.4 1.0 convolution_dynamic-update-slice_fusion.4
  376.4 2.9 convolution_subtract_fusion.5
  379.3 11.7 %cholesky.544 = f32[128,128]{1,0:T(8,128)S(1)} custom-call(f32[128,128]{1,0:T(8,128)S(1)} %cholesky.606), custom_call_target="Cholesky" | custom-call | tf_op jit(solution)/shard_map/jit(cholesky)/cholesky | solution.py:68
  391.8 9.8 %custom-call.68 = f32[1,128,128]{1,2,0:T(8,128)S(1)} custom-call(f32[1,128,128]{2,1,0:T(8,128)S(1)} %get-tuple-element.36), custom_call_target="InvertDiagBlocksLowerTriangular" | custom-call | tf_op jit(solution)/shard_map/jit(cholesky)/cholesky | solution.py:68
  401.6 0.9 convolution_dynamic-update-slice_fusion.5
  402.5 2.1 convolution_subtract_fusion.6
  404.6 11.7 %cholesky.562 = f32[128,128]{1,0:T(8,128)S(1)} custom-call(f32[128,128]{1,0:T(8,128)S(1)} %convolution_subtract_fusion.6), custom_call_target="Cholesky" | custom-call | tf_op jit(solution)/shard_map/jit(cholesky)/cholesky | solution.py:68
  426.8 6.7 %fusion.5 = (f32[1024,1024]{0,1:T(8,128)}, f32[1,1024,1024]{2,1,0:T(8,128)}) fusion(f32[1024,1024]{0,1:T(8,128)} %constant_dynamic-update-slice_fusion.30, pred[]{:T(512)S(6)} %cholesky.576), kind=kLoop, calls=%fused_computation.12 | loop fusion | flops 4194304 | bytes 12582913 | tf_op jit(solution)/shard_map/triangular_solve | solution.py:69
  433.5 24.1 %while.1 = (s32[]{:T(128)}, f32[1024,1024]{0,1:T(8,128)}, s32[8,2]{0,1:T(2,128)S(1)}, f32[8,128,128]{2,1,0:T(8,128)S(1)}, s32[]{:T(128)}) while((s32[]{:T(128)}, f32[1024,1024]{0,1:T(8,128)}, s32[8,2]{0,1:T(2,128)S(1)}, f32[8,128,128]{2,1,0:T(8,128)S(1)}, s32[]{:T(128)}) %tuple.59), condition=%wide.while_cond, body=%wide.while_body.sunk | while | flops 2 | bytes 393329 | solution.py:69
  434.3 2.3 dynamic-slice.7
  437.3 2.3 dynamic-slice.7
  440.3 2.3 dynamic-slice.7
  443.3 2.3 dynamic-slice.7
  446.3 2.3 dynamic-slice.7
  449.3 2.3 dynamic-slice.7
  452.3 2.3 dynamic-slice.7
  455.3 2.2 dynamic-slice.7
  457.6 78.6 %custom-call.69 = f32[8,128,128]{1,2,0:T(8,128)S(1)} custom-call(f32[8,128,128]{2,1,0:T(8,128)S(1)} %get-tuple-element.10), custom_call_target="InvertDiagBlocksLowerTriangular" | custom-call | tf_op jit(solution)/shard_map/triangular_solve | solution.py:69
  536.4 1.0 convolution_subtract_fusion.10
  537.6 1.1 convolution_subtract_fusion.9
  538.9 1.2 convolution_subtract_fusion.8
  540.3 1.2 convolution_subtract_fusion.7
  541.7 1.3 convolution_subtract_fusion.13
  543.1 1.3 convolution_subtract_fusion.12
  544.6 1.4 convolution_subtract_fusion.11
  546.4 7.3 %psum.15 = f32[32]{0:T(128)} all-reduce(f32[32]{0:T(128)S(1)} %broadcast_multiply_fusion), channel_id=1, replica_groups=mesh['rep'=8,'layer'=4] {'layer'}, use_global_device_ids=true, to_apply=%region_20.21 | all-reduce | flops 32 | bytes 256 | tf_op jit(solution)/shard_map/psum | solution.py:73
  (116 shorter events, 22.1 us)
Async XLA Ops:
  7.2 9.2 %copy-start = (bf16[1,32,8192]{2,1,0:T(8,128)(2,1)S(1)}, bf16[1,32,8192]{2,1,0:T(8,128)(2,1)}, u32[]{:S(2)}) copy-start(bf16[1,32,8192]{2,1,0:T(8,128)(2,1)} %param.9) | copy-start | bytes 1572868
  7.2 196.2 %all-reduce.3.cloned.1.call-start = ((), (), s32[]{:S(2)}) async-start(), calls=%async_computation | async-start | bytes 8388608 | tf_op jit(solution)/shard_map/psum | solution.py:65
  8.1 18.5 %collective-permute-start.1 = (f32[1]{0:T(128)S(1)}, f32[1]{0:T(128)}, u32[]{:S(2)}, u32[]{:S(2)}) collective-permute-start(f32[1]{0:T(128)S(1)} %bitcast.148), channel_id=1, source_target_pairs={{4,0},{8,4},{12,8},{16,12},{20,16},{24,20},{28,24},{5,1},{9,5},{13... | collective-permute-start | bytes 20 | tf_op jit(solution)/shard_map/ppermute | solution.py:15
  16.4 8.9 %copy-start.4 = (s32[512]{0:T(512)S(1)}, s32[512]{0:T(512)}, u32[]{:S(2)}) copy-start(s32[512]{0:T(512)} %param.10) | copy-start | bytes 6148
  16.4 10.2 %copy-start.5 = (s32[62]{0:T(128)S(1)}, s32[62]{0:T(128)}, u32[]{:S(2)}) copy-start(s32[62]{0:T(128)} %param.11) | copy-start | bytes 748
  23.2 7.0 %collective-permute-start = (f32[1,1024]{1,0:T(1,128)S(1)}, f32[1,1024]{1,0:T(1,128)S(1)}, u32[]{:S(2)}, u32[]{:S(2)}) collective-permute-start(f32[1,1024]{1,0:T(1,128)S(1)} %slice.248), channel_id=1, source_target_pairs={{4,0},{8,4},{12,8},{16,12},{20,16},{24,20},{28,24},{5,1},{9,5},{13... | collective-permute-start | bytes 12296 | tf_op jit(solution)/shard_map/ppermute | solution.py:15
  30.6 6.7 %collective-permute-start.3 = (bf16[32,1024]{1,0:T(8,128)(2,1)S(1)}, bf16[32,1024]{1,0:T(8,128)(2,1)S(1)}, u32[]{:S(2)}, u32[]{:S(2)}) collective-permute-start(bf16[32,1024]{1,0:T(8,128)(2,1)S(1)} %convolution_convert_fusion), channel_id=1, source_target_pairs={{0,4},{4,8},{8,12},{12,16},{16,20},{20,24},{24,28},{1,5},{5,9},{9,... | collective-permute-start | bytes 196616 | tf_op jit(solution)/shard_map/ppermute | solution.py:15
  35.6 6.2 %collective-permute-start.2 = (bf16[32,1024]{1,0:T(8,128)(2,1)S(1)}, bf16[32,1024]{1,0:T(8,128)(2,1)S(1)}, u32[]{:S(2)}, u32[]{:S(2)}) collective-permute-start(bf16[32,1024]{1,0:T(8,128)(2,1)S(1)} %convolution_convert_fusion.1), channel_id=1, source_target_pairs={{4,0},{8,4},{12,8},{16,12},{20,16},{24,20},{28,24},{5,1},{9,5},{13... | collective-permute-start | bytes 196616 | tf_op jit(solution)/shard_map/ppermute | solution.py:15
  41.9 494.4 %copy-start.3 = (bf16[32,1024]{1,0:T(8,128)(2,1)}, bf16[32,1024]{1,0:T(8,128)(2,1)S(1)}, u32[]{:S(2)}) copy-start(bf16[32,1024]{1,0:T(8,128)(2,1)S(1)} %get-tuple-element.28) | copy-start | bytes 196612
  218.4 2.0 copy-start.2
  268.3 2.0 copy-start.1
Sparse Core Ops, SparseCore 0:
  44.8 158.4 all-reduce.2
where the time goes:
time: 568 us; the launch traced here: 561 us
  other arithmetic  267 us (47%)
  waiting for transfers between devices  166 us (29%)
  matrix products  52.1 us (9%)
  local copies, waits for them, and re-layouts  39.6 us (7%)
  between operations  20.1 us (4%)
  starting transfers between devices  8.76 us (2%)
  blocking collectives  7.35 us (1%)
    another operation x30, other arithmetic, on_device(): lower = jnp.linalg.cholesky(hessian)  167 us
    psum x1, waiting for transfers between devices, on_device(): gram = lax.psum(local_gram, 'rep')  159 us
    another operation x3, other arithmetic, on_device(): lax.linalg.triangular_solve(lower, mine.T.astype(jnp.float32), left_side=...  85.3 us
    another operation x14, matrix products, on_device(): lower = jnp.linalg.cholesky(hessian)  26.2 us
    another operation x40, local copies, waits for them, and re-layouts  23.6 us
  transfers between devices with their start and end apart: 5, of which 4 were waited for; matrix products, arithmetic and copies ran while one was open for 3% of the time, Pallas kernels for 0%

commit v1 on v0

v1 whole, which is shorter than its diff:
```python
import functools

import jax
import jax.numpy as jnp
from jax import lax
from jax.experimental import pallas as pl
from jax.experimental.pallas import tpu as pltpu
from jax.sharding import PartitionSpec as P

BAL = 32
DAMPING = 0.05
BLK = 128
PAN = 256
SUP = 32
STEP = 16
EXACT = lax.Precision.HIGHEST
VMEM = pl.BlockSpec(memory_space=pltpu.VMEM)
FAR = pl.BlockSpec(memory_space=pltpu.HBM)


def swapped(block, axis, distance):
    devices = range(lax.axis_size(axis))
    return lax.ppermute(block, axis, [(i, i ^ distance) for i in devices])


def gathered(block, axis):
    even = [swapped(block, axis, d) for d in range(2, lax.axis_size(axis), 2)]
    pieces = [block, swapped(block, axis, 1)]
    for piece in even:
        pieces += [piece, swapped(piece, axis, 1)]
    return pieces


def lane_of(v, j):
    return jnp.broadcast_to(v[:, j : j + 1], v.shape)


def row_of(v, s):
    return jnp.broadcast_to(v[s : s + 1, :], v.shape)


def dot(a, b, precision=EXACT):
    return jnp.dot(a, b, precision=precision, preferred_element_type=jnp.float32)


def dot_t(a, b, precision=EXACT):
    return lax.dot_general(
        a, b, (((0,), (0,)), ((), ())), precision=precision, preferred_element_type=jnp.float32
    )


def dot_n(a, b):
    return lax.dot_general(a, b, (((1,), (1,)), ((), ())), preferred_element_type=jnp.float32)


def project_kernel(acts, grads, w_in, w_out, segments, moves, out, a_ref, g_ref, wi_ref, wo_ref, seg_ref, move_ref, sems):
    tokens, depth = a_ref.shape
    parts = sems.shape[0] // 2 - 2
    deep = depth // parts
    width = w_in.shape[0]
    small = [
        pltpu.make_async_copy(segments, seg_ref, sems.at[2 * parts]),
        pltpu.make_async_copy(moves, move_ref, sems.at[2 * parts + 1]),
    ]
    weights = [
        pltpu.make_async_copy(w_in, wi_ref, sems.at[2 * parts + 2]),
        pltpu.make_async_copy(w_out, wo_ref, sems.at[2 * parts + 3]),
    ]
    copies = []
    for c in range(parts):
        at = pl.ds(c * deep, deep)
        copies += [
            pltpu.make_async_copy(acts.at[:, at], a_ref.at[:, at], sems.at[2 * c]),
            pltpu.make_async_copy(grads.at[:, at], g_ref.at[:, at], sems.at[2 * c + 1]),
        ]
    for copy in [*small, *weights, *copies]:
        copy.start()
    for copy in small:
        copy.wait()
    slots = moves.shape[1]
    slot = lax.broadcasted_iota(jnp.int32, (slots, slots), 0)
    other = lax.broadcasted_iota(jnp.int32, (slots, slots), 1)
    column = jnp.sum(jnp.where(slot == other, move_ref[...], 0), axis=1, keepdims=True)
    segment = seg_ref[...]
    slot = lax.broadcasted_iota(jnp.int32, (slots, tokens), 0)
    target = jnp.sum(jnp.where(slot == segment, column, 0), axis=0, keepdims=True)
    target = jnp.where(segment < 0, -1, target)
    line = lax.broadcasted_iota(jnp.int32, (16, tokens), 0)
    coded = jnp.where(line == 0, target >> 5, jnp.where(line == 1, target & 31, 0))
    out[2 * width :, :] = coded.astype(jnp.float32).astype(jnp.bfloat16)
    for copy in weights:
        copy.wait()
    left = right = jnp.zeros((tokens, width), jnp.float32)
    for c in range(parts):
        at = slice(c * deep, c * deep + deep)
        copies[2 * c].wait()
        copies[2 * c + 1].wait()
        left = left + dot_n(a_ref[:, at], wi_ref[:, at])
        right = right + dot_n(g_ref[:, at], wo_ref[:, at])
    out[0:width, :] = left.T.astype(jnp.bfloat16)
    out[width : 2 * width, :] = right.T.astype(jnp.bfloat16)


def project(activations, output_grads, in_projection, out_projection, segment_ids, move_list):
    tokens, depth = activations.shape
    width = in_projection.shape[0]
    slots = move_list.shape[0]
    parts = depth // 512
    return pl.pallas_call(
        project_kernel,
        out_shape=jax.ShapeDtypeStruct((2 * width + 16, tokens), jnp.bfloat16),
        in_specs=[FAR] * 6,
        out_specs=VMEM,
        scratch_shapes=[
            pltpu.VMEM((tokens, depth), jnp.bfloat16),
            pltpu.VMEM((tokens, depth), jnp.bfloat16),
            pltpu.VMEM((width, depth), jnp.bfloat16),
            pltpu.VMEM((width, depth), jnp.bfloat16),
            pltpu.VMEM((1, tokens), jnp.int32),
            pltpu.VMEM((1, slots), jnp.int32),
            pltpu.SemaphoreType.DMA((2 * parts + 4,)),
        ],
        compiler_params=pltpu.CompilerParams(vmem_limit_bytes=58 * 1024 * 1024),
        name="project",
    )(
        activations,
        output_grads,
        in_projection,
        out_projection,
        segment_ids.reshape(1, tokens),
        move_list.reshape(1, slots),
    )


def eliminate(x, first):
    lane = lax.broadcasted_iota(jnp.int32, (8, BLK), 1)
    sub = lax.broadcasted_iota(jnp.int32, (8, BLK), 0)
    x, count, deep = list(x), len(x), STEP // 8
    scales = [None] * count
    for t in range(0, count, deep):
        lo = first + 8 * t
        cols = [[lane_of(x[t + q], lo + c) for q in range(deep)] for c in range(STEP)]
        below = {i: [lane_of(x[i], lo + c) for c in range(STEP)] for i in range(t + deep, count)}
        work = [x[t + q] for q in range(deep)]
        kept, pivots = list(work), [jnp.ones((8, BLK), jnp.float32)] * deep
        for c in range(STEP):
            own, s = divmod(c, 8)
            hit, at = sub == s, lane == lo + c
            pivot = row_of(cols[c][own], s)
            inv = 1.0 / pivot
            kept[own] = jnp.where(hit, work[own], kept[own])
            pivots[own] = jnp.where(hit, pivot, pivots[own])
            row = jnp.where(at, 1.0, row_of(work[own], s)) * inv
            for q in range(deep):
                new = jnp.where(at, 0.0, work[q]) - cols[c][q] * row
                work[q] = jnp.where(hit, row, new) if q == own else new
            for k in range(c + 1, STEP):
                raw = row_of(cols[k][own], s)
                weight = raw * inv
                for q in range(deep):
                    if k == c + 1:
                        new = cols[k][q] - (cols[c][q] * raw) * inv
                    else:
                        new = cols[k][q] - cols[c][q] * weight
                    cols[k][q] = jnp.where(hit, weight, new) if q == own else new
        inside = (lane >= lo) & (lane < lo + STEP)
        for i in range(t + deep, count):
            terms = [below[i][c] * row_of(work[c // 8], c % 8) for c in range(STEP)]
            while len(terms) > 1:
                terms = [terms[m] + terms[m + 1] for m in range(0, len(terms), 2)]
            x[i] = jnp.where(inside, 0.0, x[i]) - terms[0]
        for q in range(deep):
            scales[t + q] = lax.rsqrt(pivots[q])
            x[t + q] = kept[q] * scales[t + q]
    return x, scales


def factor_block(d_ref, u_ref, m_ref):
    lane = lax.broadcasted_iota(jnp.int32, (8, BLK), 1)
    sub = lax.broadcasted_iota(jnp.int32, (8, BLK), 0)
    tall_row = lax.broadcasted_iota(jnp.int32, (SUP, BLK), 0)
    tall_lane = lax.broadcasted_iota(jnp.int32, (SUP, BLK), 1)
    groups, n = BLK // 8, SUP // 8
    x = [d_ref[8 * i : 8 * i + 8, :] for i in range(groups)]
    for h in range(0, groups, n):
        a, b = 8 * h, 8 * (h + n)
        rows, scales = eliminate(x[h : h + n], a)
        if b < BLK:
            block, scale = jnp.concatenate(rows, 0), jnp.concatenate(scales, 0)
            row = tall_row + a
            right = jnp.where(
                (tall_lane > row) & (tall_lane < b), 0.0, jnp.where(tall_lane == row, scale, block)
            )
            update = dot_t(block, right)
            for i in range(h + n, groups):
                x[i] = jnp.where((lane >= a) & (lane < b), 0.0, x[i]) - update[8 * i : 8 * i + 8, :]
        for q in range(n):
            row = a + 8 * q + sub
            at = slice(a + 8 * q, a + 8 * q + 8)
            u_ref[at, :] = jnp.where(lane >= row, rows[q], 0.0)
            m_ref[at, :] = jnp.where(lane < row, rows[q], jnp.where(lane == row, scales[q], 0.0))


def factor_kernel(width, me_ref, *refs):
    *pieces, u_out, mine_out, quad_ref, tok_ref, sum_ref, len_ref, p_ref, f_ref, u_ref, s_ref, d_ref, m_ref, sems = refs
    n_rep = len(pieces)
    docs = p_ref.shape[0]
    rows = docs // n_rep
    tokens = p_ref.shape[1]
    me = me_ref[0]
    for d in range(n_rep):
        tok_ref[me ^ d] = pieces[d][...]
    sum_ref[...] = jnp.zeros_like(sum_ref)
    len_ref[...] = jnp.zeros_like(len_ref)
    side = (tok_ref.shape[1] - 16) // 2
    doc = lax.broadcasted_iota(jnp.int32, (docs, tokens), 0).astype(jnp.float32)
    ones = jnp.ones((16, tokens), jnp.bfloat16)
    tall = 8 * side

    def add_tokens(r, last):
        left = tok_ref[r, 0:side, :].astype(jnp.float32)
        right = tok_ref[r, side : 2 * side, :].astype(jnp.float32)
        coded = tok_ref[r, 2 * side :, :].astype(jnp.float32)
        target = coded[0:1, :] * 32.0 + coded[1:2, :]
        target = jnp.where(target < 0.0, last, target)
        p_ref[...] = jnp.where(doc == target, 1.0, 0.0).astype(jnp.bfloat16)
        len_ref[...] += dot_n(ones, p_ref[...])
        for q in range(0, side, 8):
            outer = jnp.concatenate(
                [jnp.broadcast_to(left[i : i + 1, :], right.shape) * right for i in range(q, q + 8)], 0
            )
            high = outer.astype(jnp.bfloat16)
            low = (outer - high.astype(jnp.float32)).astype(jnp.bfloat16)
            sum_ref[q * side : q * side + tall, :] += dot_n(high, p_ref[...]) + dot_n(low, p_ref[...])
        return target[:, tokens - 1 : tokens]

    lax.fori_loop(0, n_rep, add_tokens, jnp.zeros((1, 1), jnp.float32))
    scale = lax.rsqrt(jnp.maximum(len_ref[0:1, :], 1.0))
    f_ref[...] = (sum_ref[...] * scale).astype(jnp.bfloat16)
    row = lax.broadcasted_iota(jnp.int32, (docs, BLK), 0)
    slot = lax.broadcasted_iota(jnp.int32, (docs, BLK), 1)
    pick = jnp.where((row == me * rows + slot) & (slot < rows), 1.0, 0.0).astype(jnp.bfloat16)
    row = lax.broadcasted_iota(jnp.int32, (rows, docs), 0)
    slot = lax.broadcasted_iota(jnp.int32, (rows, docs), 1)
    pick_t = jnp.where(slot == me * rows + row, 1.0, 0.0).astype(jnp.bfloat16)
    mine_out[...] = dot_n(pick_t, f_ref[...]).astype(jnp.bfloat16)
    eye = jnp.where(
        lax.broadcasted_iota(jnp.int32, (PAN, PAN), 0) == lax.broadcasted_iota(jnp.int32, (PAN, PAN), 1),
        DAMPING,
        0.0,
    )

    def start_panel(k):
        a, c = PAN * k, PAN * k + PAN
        gram = dot_n(f_ref[a:c, :], f_ref[a:, :]) * (1.0 / docs)
        own = dot(f_ref[a:c, :], pick, None)
        if k:
            done = u_ref[0:a, a:c]
            gram = gram - dot_t(done, u_ref[0:a, a:width])
            own = own - dot_t(done, u_ref[0:a, width:])
            u_ref[a:c, 0:a] = jnp.zeros((PAN, a), jnp.float32)
        u_ref[a + BLK : c, a : a + BLK] = jnp.zeros((BLK, BLK), jnp.float32)
        s_ref[:, a:c] = gram[:, 0:PAN] + eye
        if c < width:
            s_ref[:, c:width] = gram[:, PAN:]
        s_ref[:, width:] = own
        d_ref[...] = s_ref[0:BLK, a : a + BLK]

    def first_half(k):
        a, b, c = PAN * k, PAN * k + BLK, PAN * k + PAN
        upper = dot(m_ref[...], s_ref[0:BLK, b:])
        u_ref[a:b, b:] = upper
        update = dot_t(upper[:, 0:BLK], upper)
        d_ref[...] = s_ref[BLK:, b:c] - update[:, 0:BLK]
        s_ref[BLK:, c:] = s_ref[BLK:, c:] - update[:, BLK:]

    def panel_copy(k):
        at = pl.ds(PAN * k, PAN)
        return pltpu.make_async_copy(u_ref.at[at, 0:width], u_out.at[at, :], sems.at[k])

    def second_half(k):
        b, c = PAN * k + BLK, PAN * k + PAN
        u_ref[b:c, c:] = dot(m_ref[...], s_ref[BLK:, c:])
        panel_copy(k).start()
        if c < width:
            start_panel(k + 1)

    start_panel(0)

    def block(m, carry):
        at = pl.ds(pl.multiple_of(m * BLK, BLK), BLK)
        factor_block(d_ref, u_ref.at[at, at], m_ref)
        for i in range(width // BLK):

            @pl.when(m == i)
            def _():
                (second_half if i % 2 else first_half)(i // 2)

        return carry

    lax.fori_loop(0, width // BLK, block, 0)
    solved = u_ref[:, width:]
    quad = jnp.sum(solved * solved, axis=0, keepdims=True) * (1.0 / width)
    quad_ref[...] = quad
    for k in range(width // PAN):
        panel_copy(k).wait()


def factor_and_solve(pieces, replica):
    n_rep = len(pieces)
    height, tokens = pieces[0].shape
    width = ((height - 16) // 2) ** 2
    docs = n_rep * BAL
    return pl.pallas_call(
        functools.partial(factor_kernel, width),
        out_shape=[
            jax.ShapeDtypeStruct((width, width), jnp.float32),
            jax.ShapeDtypeStruct((BAL, width), jnp.bfloat16),
            jax.ShapeDtypeStruct((1, BLK), jnp.float32),
        ],
        in_specs=[pl.BlockSpec(memory_space=pltpu.SMEM)] + [VMEM] * n_rep,
        out_specs=[pl.BlockSpec(memory_space=pl.ANY), VMEM, VMEM],
        scratch_shapes=[
            pltpu.VMEM((n_rep, height, tokens), jnp.bfloat16),
            pltpu.VMEM((width, docs), jnp.float32),
            pltpu.VMEM((16, docs), jnp.float32),
            pltpu.VMEM((docs, tokens), jnp.bfloat16),
            pltpu.VMEM((width, docs), jnp.bfloat16),
            pltpu.VMEM((width, width + BLK), jnp.float32),
            pltpu.VMEM((PAN, width + BLK), jnp.float32),
            pltpu.VMEM((BLK, BLK), jnp.float32),
            pltpu.VMEM((BLK, BLK), jnp.float32),
            pltpu.SemaphoreType.DMA((width // PAN,)),
        ],
        compiler_params=pltpu.CompilerParams(vmem_limit_bytes=48 * 1024 * 1024),
        name="factor",
    )(jnp.reshape(replica, (1,)).astype(jnp.int32), *pieces)


def on_device(activations, output_grads, in_projection, out_projection, segment_ids, move_list):
    tokens = project(
        activations[0], output_grads[0], in_projection[0], out_projection[0], segment_ids, move_list
    )
    upper, mine, quad = factor_and_solve(gathered(tokens, "rep"), lax.axis_index("rep"))
    layers = [quad] + [swapped(quad, "layer", d) for d in range(1, lax.axis_size("layer"))]
    while len(layers) > 1:
        layers = [layers[i] + layers[i + 1] for i in range(0, len(layers), 2)]
    return (upper[None], mine[None], layers[0][0, :BAL])


def solution(mesh):
    placed = (
        P("layer", "rep", None),
        P("layer", "rep", None),
        P("layer", None, None),
        P("layer", None, None),
        P("rep"),
        P("rep"),
    )
    return jax.shard_map(
        on_device,
        mesh=mesh,
        in_specs=placed,
        out_specs=(P("layer", None, None), P("layer", "rep", None), P("rep")),
        check_vma=False,
    )
```

time: 568 us -> 77 us (0.14); the launches traced: 561 us -> 76.8 us
  other arithmetic: 267 us -> 0.01 us
  waiting for transfers between devices: 166 us -> 8.7 us
  Pallas kernels: 0 us -> 52.9 us
  matrix products: 52.1 us -> 0 us
  local copies, waits for them, and re-layouts: 39.6 us -> 1.4 us
  between operations: 20.1 us -> 0.66 us
  blocking collectives: 7.35 us -> 0 us
    another operation x33 -> x0, other arithmetic: 253 us -> none  [the longest x30 167 us: on_device(): lower = jnp.linalg.cholesky(hessian)]
    psum x1 -> x0, waiting for transfers between devices: 159 us -> none  [on_device(): gram = lax.psum(local_gram, 'rep')]
    pallas_call x0 -> x2, Pallas kernels: none -> 52.9 us  [the longest x1 45.2 us: factor_and_solve(): pl.pallas_call(functools.partial(factor_kernel, width), out_shape=[jax.Sh...]
    another operation x29 -> x0, matrix products: 36 us -> none  [the longest x14 26.2 us: on_device(): lower = jnp.linalg.cholesky(hessian)]
    another operation x66 -> x0, local copies, waits for them, and re-layouts: 29.2 us -> none
    dot_general x6 -> x0, matrix products: 16.1 us -> none  [the longest x1 6.67 us: on_device(): lax.dot_general(masked, right, (((2,), (1,)), ((), ())), preferred_elemen...]
    psum x1 -> x0, blocking collectives: 7.35 us -> none  [on_device(): influence = lax.psum(quad, 'layer')]
    ppermute x4 -> x10, starting transfers between devices: 8.73 us -> 13.1 us  [swapped(): return lax.ppermute(block, axis, [(i, i ^ distance) for i in devices])]
  transfers between devices with their start and end apart: 5 -> 10, of which waited for: 4 -> 6; matrix products, arithmetic and copies ran while one was open for 3% -> 0% of each run, Pallas kernels for 0% -> 0%
where the time goes in v1:
time: 77 us; the launch traced here: 76.8 us
  Pallas kernels  52.9 us (69%)
  starting transfers between devices  13.1 us (17%)
  waiting for transfers between devices  8.7 us (11%)
  local copies, waits for them, and re-layouts  1.4 us (2%)
    pallas_call x1, Pallas kernels, factor_and_solve(): pl.pallas_call(functools.partial(factor_kernel, width), out_shape=[jax.Sh...  45.2 us
    ppermute x10, starting transfers between devices, swapped(): return lax.ppermute(block, axis, [(i, i ^ distance) for i in devices])  13.1 us
    ppermute x10, waiting for transfers between devices, swapped(): return lax.ppermute(block, axis, [(i, i ^ distance) for i in devices])  8.7 us
    pallas_call x1, Pallas kernels, project(): pl.pallas_call(project_kernel, out_shape=jax.ShapeDtypeStruct((2 * width...  7.7 us
  transfers between devices with their start and end apart: 10, of which 6 were waited for; matrix products, arithmetic and copies ran while one was open for 0% of the time, Pallas kernels for 0%

profile of v1, /device:TPU:0, one launch (start us, length us, event | category | flops | bytes accessed | tf_op | source)
XLA Modules:
  0.0 76.8 jit_solution(10628685305681559963)
XLA Ops:
  0.6 7.7 %project.1.refs_0_ = bf16[80,512]{1,0:T(8,128)(2,1)} custom-call(bf16[512,8192]{1,0:T(8,128)(2,1)} %bitcast.11, bf16[512,8192]{1,0:T(8,128)(2,1)} %bitcast.12, bf16[32,8192]{1,0:T(8,128)(2,1)} %bitcast.13, bf16[32,8192]{1,0:T(8,128)(2,1)} %bitcast.14, s32[1,512]{1,0:T(1,128)} %bitcast.15, s32[1,62]{1,0:T(1,128)} %bitcast.16), custom_call_target="tpu_custom_call" | custom-call | tf_op jit(solution)/shard_map/project/pallas_call | solution.py:109
  8.3 5.1 %collective-permute-start.5 = (bf16[80,512]{1,0:T(8,128)(2,1)}, bf16[80,512]{1,0:T(8,128)(2,1)S(1)}, u32[]{:S(2)}, u32[]{:S(2)}) collective-permute-start(bf16[80,512]{1,0:T(8,128)(2,1)} %project.1.refs_0_), channel_id=1, source_target_pairs={{0,24},{4,28},{8,16},{12,20},{16,8},{20,12},{24,0},{28,4},{1,25},{... | collective-permute-start | bytes 245768 | tf_op jit(solution)/shard_map/ppermute | solution.py:23
  13.4 0.0 collective-permute-start.3
  13.4 0.6 collective-permute-start.1
  14.1 1.6 %collective-permute-start = (bf16[80,512]{1,0:T(8,128)(2,1)}, bf16[80,512]{1,0:T(8,128)(2,1)S(1)}, u32[]{:S(2)}, u32[]{:S(2)}) collective-permute-start(bf16[80,512]{1,0:T(8,128)(2,1)} %project.1.refs_0_), channel_id=1, source_target_pairs={{0,4},{4,0},{8,12},{12,8},{16,20},{20,16},{24,28},{28,24},{1,5},{5... | collective-permute-start | bytes 245768 | tf_op jit(solution)/shard_map/ppermute | solution.py:23
  15.7 1.0 %collective-permute-done.5.refs_6_ = bf16[80,512]{1,0:T(8,128)(2,1)S(1)} collective-permute-done((bf16[80,512]{1,0:T(8,128)(2,1)}, bf16[80,512]{1,0:T(8,128)(2,1)S(1)}, u32[]{:S(2)}, u32[]{:S(2)}) %collective-permute-start.5) | collective-permute-done | bytes 81952 | tf_op jit(solution)/shard_map/ppermute | solution.py:23
  16.7 1.8 %collective-permute-start.6 = (bf16[80,512]{1,0:T(8,128)(2,1)S(1)}, bf16[80,512]{1,0:T(8,128)(2,1)S(1)}, u32[]{:S(2)}, u32[]{:S(2)}) collective-permute-start(bf16[80,512]{1,0:T(8,128)(2,1)S(1)} %collective-permute-done.5.refs_6_), channel_id=1, source_target_pairs={{0,4},{4,0},{8,12},{12,8},{16,20},{20,16},{24,28},{28,24},{1,5},{5... | collective-permute-start | bytes 245768 | tf_op jit(solution)/shard_map/ppermute | solution.py:23
  18.4 2.1 %collective-permute-done.3.refs_4_ = bf16[80,512]{1,0:T(8,128)(2,1)S(1)} collective-permute-done((bf16[80,512]{1,0:T(8,128)(2,1)}, bf16[80,512]{1,0:T(8,128)(2,1)S(1)}, u32[]{:S(2)}, u32[]{:S(2)}) %collective-permute-start.3) | collective-permute-done | bytes 81952 | tf_op jit(solution)/shard_map/ppermute | solution.py:23
  20.5 1.5 %collective-permute-start.4 = (bf16[80,512]{1,0:T(8,128)(2,1)S(1)}, bf16[80,512]{1,0:T(8,128)(2,1)S(1)}, u32[]{:S(2)}, u32[]{:S(2)}) collective-permute-start(bf16[80,512]{1,0:T(8,128)(2,1)S(1)} %collective-permute-done.3.refs_4_), channel_id=1, source_target_pairs={{0,4},{4,0},{8,12},{12,8},{16,20},{20,16},{24,28},{28,24},{1,5},{5... | collective-permute-start | bytes 245768 | tf_op jit(solution)/shard_map/ppermute | solution.py:23
  22.0 0.0 collective-permute-done.1.refs_2_
  22.0 0.5 collective-permute-start.2
  22.5 0.0 collective-permute-done.refs_1_
  22.6 0.0 collective-permute-done.6.refs_7_
  22.6 3.0 %collective-permute-done.4.refs_5_ = bf16[80,512]{1,0:T(8,128)(2,1)S(1)} collective-permute-done((bf16[80,512]{1,0:T(8,128)(2,1)S(1)}, bf16[80,512]{1,0:T(8,128)(2,1)S(1)}, u32[]{:S(2)}, u32[]{:S(2)}) %collective-permute-start.4) | collective-permute-done | bytes 81952 | tf_op jit(solution)/shard_map/ppermute | solution.py:23
  25.5 0.9 %collective-permute-done.2.refs_3_ = bf16[80,512]{1,0:T(8,128)(2,1)S(1)} collective-permute-done((bf16[80,512]{1,0:T(8,128)(2,1)S(1)}, bf16[80,512]{1,0:T(8,128)(2,1)S(1)}, u32[]{:S(2)}, u32[]{:S(2)}) %collective-permute-start.2) | collective-permute-done | bytes 81952 | tf_op jit(solution)/shard_map/ppermute | solution.py:23
  26.5 0.0 copy-start
  26.5 0.9 %copy-done = bf16[80,512]{1,0:T(8,128)(2,1)S(1)} copy-done((bf16[80,512]{1,0:T(8,128)(2,1)S(1)}, bf16[80,512]{1,0:T(8,128)(2,1)}, u32[]{:S(2)}) %copy-start) | copy-done | bytes 81944
  27.3 45.2 %factor.1 = (f32[1024,1024]{1,0:T(8,128)}, bf16[32,1024]{1,0:T(8,128)(2,1)}, f32[1,128]{1,0:T(1,128)S(1)}) custom-call(s32[1]{0:T(128)} %bitcast.me_ref, bf16[80,512]{1,0:T(8,128)(2,1)S(1)} %copy-done, bf16[80,512]{1,0:T(8,128)(2,1)S(1)} %collective-permute-done.refs_1_, bf16[80,512]{1,0:T(8,128)(2,1)S(1)} %collective-permute-done.1.refs_2_, ...), custom_call_target="tpu_custom_call" | custom-call | tf_op jit(solution)/shard_map/factor/pallas_call | solution.py:314
  72.6 0.1 collective-permute-start.9
  72.7 1.6 %collective-permute-start.8 = (f32[1,128]{1,0:T(1,128)S(1)}, f32[1,128]{1,0:T(1,128)S(1)}, u32[]{:S(2)}, u32[]{:S(2)}) collective-permute-start(f32[1,128]{1,0:T(1,128)S(1)} %get-tuple-element.8), channel_id=1, source_target_pairs={{0,2},{1,3},{2,0},{3,1},{4,6},{5,7},{6,4},{7,5},{8,10},{9,11},{10,... | collective-permute-start | bytes 1544 | tf_op jit(solution)/shard_map/ppermute | solution.py:23
  74.2 0.3 collective-permute-start.7
  74.5 1.1 %collective-permute-done.9 = f32[1,128]{1,0:T(1,128)S(1)} collective-permute-done((f32[1,128]{1,0:T(1,128)S(1)}, f32[1,128]{1,0:T(1,128)S(1)}, u32[]{:S(2)}, u32[]{:S(2)}) %collective-permute-start.9) | collective-permute-done | bytes 544 | tf_op jit(solution)/shard_map/ppermute | solution.py:23
  75.6 0.7 collective-permute-done.8
  76.3 0.0 collective-permute-done.7
  76.3 0.5 slice_bitcast_fusion
  (1 shorter events, 0.0 us)
Async XLA Ops:
  8.3 8.3 %collective-permute-start.5 = (bf16[80,512]{1,0:T(8,128)(2,1)}, bf16[80,512]{1,0:T(8,128)(2,1)S(1)}, u32[]{:S(2)}, u32[]{:S(2)}) collective-permute-start(bf16[80,512]{1,0:T(8,128)(2,1)} %project.1.refs_0_), channel_id=1, source_target_pairs={{0,24},{4,28},{8,16},{12,20},{16,8},{20,12},{24,0},{28,4},{1,25},{... | collective-permute-start | bytes 245768 | tf_op jit(solution)/shard_map/ppermute | solution.py:23
  13.4 7.1 %collective-permute-start.3 = (bf16[80,512]{1,0:T(8,128)(2,1)}, bf16[80,512]{1,0:T(8,128)(2,1)S(1)}, u32[]{:S(2)}, u32[]{:S(2)}) collective-permute-start(bf16[80,512]{1,0:T(8,128)(2,1)} %project.1.refs_0_), channel_id=1, source_target_pairs={{0,16},{4,20},{8,24},{12,28},{16,0},{20,4},{24,8},{28,12},{1,17},{... | collective-permute-start | bytes 245768 | tf_op jit(solution)/shard_map/ppermute | solution.py:23
  13.4 8.6 %collective-permute-start.1 = (bf16[80,512]{1,0:T(8,128)(2,1)}, bf16[80,512]{1,0:T(8,128)(2,1)S(1)}, u32[]{:S(2)}, u32[]{:S(2)}) collective-permute-start(bf16[80,512]{1,0:T(8,128)(2,1)} %project.1.refs_0_), channel_id=1, source_target_pairs={{0,8},{4,12},{8,0},{12,4},{16,24},{20,28},{24,16},{28,20},{1,9},{5... | collective-permute-start | bytes 245768 | tf_op jit(solution)/shard_map/ppermute | solution.py:23
  14.1 8.5 %collective-permute-start = (bf16[80,512]{1,0:T(8,128)(2,1)}, bf16[80,512]{1,0:T(8,128)(2,1)S(1)}, u32[]{:S(2)}, u32[]{:S(2)}) collective-permute-start(bf16[80,512]{1,0:T(8,128)(2,1)} %project.1.refs_0_), channel_id=1, source_target_pairs={{0,4},{4,0},{8,12},{12,8},{16,20},{20,16},{24,28},{28,24},{1,5},{5... | collective-permute-start | bytes 245768 | tf_op jit(solution)/shard_map/ppermute | solution.py:23
  16.7 5.9 %collective-permute-start.6 = (bf16[80,512]{1,0:T(8,128)(2,1)S(1)}, bf16[80,512]{1,0:T(8,128)(2,1)S(1)}, u32[]{:S(2)}, u32[]{:S(2)}) collective-permute-start(bf16[80,512]{1,0:T(8,128)(2,1)S(1)} %collective-permute-done.5.refs_6_), channel_id=1, source_target_pairs={{0,4},{4,0},{8,12},{12,8},{16,20},{20,16},{24,28},{28,24},{1,5},{5... | collective-permute-start | bytes 245768 | tf_op jit(solution)/shard_map/ppermute | solution.py:23
  20.5 5.0 %collective-permute-start.4 = (bf16[80,512]{1,0:T(8,128)(2,1)S(1)}, bf16[80,512]{1,0:T(8,128)(2,1)S(1)}, u32[]{:S(2)}, u32[]{:S(2)}) collective-permute-start(bf16[80,512]{1,0:T(8,128)(2,1)S(1)} %collective-permute-done.3.refs_4_), channel_id=1, source_target_pairs={{0,4},{4,0},{8,12},{12,8},{16,20},{20,16},{24,28},{28,24},{1,5},{5... | collective-permute-start | bytes 245768 | tf_op jit(solution)/shard_map/ppermute | solution.py:23
  22.0 4.4 %collective-permute-start.2 = (bf16[80,512]{1,0:T(8,128)(2,1)S(1)}, bf16[80,512]{1,0:T(8,128)(2,1)S(1)}, u32[]{:S(2)}, u32[]{:S(2)}) collective-permute-start(bf16[80,512]{1,0:T(8,128)(2,1)S(1)} %collective-permute-done.1.refs_2_), channel_id=1, source_target_pairs={{0,4},{4,0},{8,12},{12,8},{16,20},{20,16},{24,28},{28,24},{1,5},{5... | collective-permute-start | bytes 245768 | tf_op jit(solution)/shard_map/ppermute | solution.py:23
  26.5 0.9 %copy-start = (bf16[80,512]{1,0:T(8,128)(2,1)S(1)}, bf16[80,512]{1,0:T(8,128)(2,1)}, u32[]{:S(2)}) copy-start(bf16[80,512]{1,0:T(8,128)(2,1)} %project.1.refs_0_) | copy-start | bytes 245764
  72.6 3.0 %collective-permute-start.9 = (f32[1,128]{1,0:T(1,128)S(1)}, f32[1,128]{1,0:T(1,128)S(1)}, u32[]{:S(2)}, u32[]{:S(2)}) collective-permute-start(f32[1,128]{1,0:T(1,128)S(1)} %get-tuple-element.8), channel_id=1, source_target_pairs={{0,3},{1,2},{2,1},{3,0},{4,7},{5,6},{6,5},{7,4},{8,11},{9,10},{10,... | collective-permute-start | bytes 1544 | tf_op jit(solution)/shard_map/ppermute | solution.py:23
  72.7 3.6 %collective-permute-start.8 = (f32[1,128]{1,0:T(1,128)S(1)}, f32[1,128]{1,0:T(1,128)S(1)}, u32[]{:S(2)}, u32[]{:S(2)}) collective-permute-start(f32[1,128]{1,0:T(1,128)S(1)} %get-tuple-element.8), channel_id=1, source_target_pairs={{0,2},{1,3},{2,0},{3,1},{4,6},{5,7},{6,4},{7,5},{8,10},{9,11},{10,... | collective-permute-start | bytes 1544 | tf_op jit(solution)/shard_map/ppermute | solution.py:23
  74.2 2.0 %collective-permute-start.7 = (f32[1,128]{1,0:T(1,128)S(1)}, f32[1,128]{1,0:T(1,128)S(1)}, u32[]{:S(2)}, u32[]{:S(2)}) collective-permute-start(f32[1,128]{1,0:T(1,128)S(1)} %get-tuple-element.8), channel_id=1, source_target_pairs={{0,1},{1,0},{2,3},{3,2},{4,5},{5,4},{6,7},{7,6},{8,9},{9,8},{10,11... | collective-permute-start | bytes 1544 | tf_op jit(solution)/shard_map/ppermute | solution.py:23

commit v2 on v1

--- a/solution.py
+++ b/solution.py
@@ -11,8 +11,7 @@
 DAMPING = 0.05
 BLK = 128
 PAN = 256
-SUP = 32
-STEP = 16
+SUP = 64
 EXACT = lax.Precision.HIGHEST
 VMEM = pl.BlockSpec(memory_space=pltpu.VMEM)
 FAR = pl.BlockSpec(memory_space=pltpu.HBM)
@@ -32,7 +31,7 @@
 
 
 def lane_of(v, j):
-    return jnp.broadcast_to(v[:, j : j + 1], v.shape)
+    return jnp.take_along_axis(v, jnp.full(v.shape, j, jnp.int32), axis=1)
 
 
 def row_of(v, s):
@@ -135,43 +134,57 @@
 def eliminate(x, first):
     lane = lax.broadcasted_iota(jnp.int32, (8, BLK), 1)
     sub = lax.broadcasted_iota(jnp.int32, (8, BLK), 0)
-    x, count, deep = list(x), len(x), STEP // 8
+    x, count = list(x), len(x)
     scales = [None] * count
-    for t in range(0, count, deep):
+    spread = lambda group, lo: [lane_of(group, lo + c) for c in range(8)]
+    cols = spread(x[0], first)
+    for t in range(count):
         lo = first + 8 * t
-        cols = [[lane_of(x[t + q], lo + c) for q in range(deep)] for c in range(STEP)]
-        below = {i: [lane_of(x[i], lo + c) for c in range(STEP)] for i in range(t + deep, count)}
-        work = [x[t + q] for q in range(deep)]
-        kept, pivots = list(work), [jnp.ones((8, BLK), jnp.float32)] * deep
-        for c in range(STEP):
-            own, s = divmod(c, 8)
-            hit, at = sub == s, lane == lo + c
-            pivot = row_of(cols[c][own], s)
+        work = x[t]
+        more = t + 1 < count
+        if more:
+            below = [spread(x[i], lo) for i in range(t + 1, count)]
+            side = spread(x[t], lo + 8)
+            ahead = spread(x[t + 1], lo + 8)
+            factor = list(below[0])
+        kept, pivots = work, jnp.ones((8, BLK), jnp.float32)
+        for c in range(8):
+            hit, at = sub == c, lane == lo + c
+            pivot = row_of(cols[c], c)
             inv = 1.0 / pivot
-            kept[own] = jnp.where(hit, work[own], kept[own])
-            pivots[own] = jnp.where(hit, pivot, pivots[own])
-            row = jnp.where(at, 1.0, row_of(work[own], s)) * inv
-            for q in range(deep):
-                new = jnp.where(at, 0.0, work[q]) - cols[c][q] * row
-                work[q] = jnp.where(hit, row, new) if q == own else new
-            for k in range(c + 1, STEP):
-                raw = row_of(cols[k][own], s)
+            kept = jnp.where(hit, work, kept)
+            pivots = jnp.where(hit, pivot, pivots)
+            row = jnp.where(at, 1.0, row_of(work, c)) * inv
+            work = jnp.where(hit, row, jnp.where(at, 0.0, work) - cols[c] * row)
+            under = jnp.where(sub > c, cols[c], 0.0)
+            for k in range(c + 1, 8):
+                raw = row_of(cols[k], c)
                 weight = raw * inv
-                for q in range(deep):
-                    if k == c + 1:
-                        new = cols[k][q] - (cols[c][q] * raw) * inv
-                    else:
-                        new = cols[k][q] - cols[c][q] * weight
-                    cols[k][q] = jnp.where(hit, weight, new) if q == own else new
-        inside = (lane >= lo) & (lane < lo + STEP)
-        for i in range(t + deep, count):
-            terms = [below[i][c] * row_of(work[c // 8], c % 8) for c in range(STEP)]
-            while len(terms) > 1:
-                terms = [terms[m] + terms[m + 1] for m in range(0, len(terms), 2)]
-            x[i] = jnp.where(inside, 0.0, x[i]) - terms[0]
-        for q in range(deep):
-            scales[t + q] = lax.rsqrt(pivots[q])
-            x[t + q] = kept[q] * scales[t + q]
+                if k == c + 1:
+                    new = cols[k] - (cols[c] * raw) * inv
+                else:
+                    new = cols[k] - cols[c] * weight
+                cols[k] = jnp.where(hit, weight, new)
+                if more:
+                    factor[k] = factor[k] - factor[c] * weight
+            if more:
+                for k in range(8):
+                    raw = row_of(side[k], c)
+                    weight = raw * inv
+                    if c < 7:
+                        side[k] = side[k] - under * weight
+                    ahead[k] = ahead[k] - factor[c] * weight
+        if more:
+            inside = (lane >= lo) & (lane < lo + 8)
+            rows = [row_of(work, c) for c in range(8)]
+            for i in range(t + 1, count):
+                terms = [below[i - t - 1][c] * rows[c] for c in range(8)]
+                while len(terms) > 1:
+                    terms = [terms[m] + terms[m + 1] for m in range(0, len(terms), 2)]
+                x[i] = jnp.where(inside, 0.0, x[i]) - terms[0]
+            cols = ahead
+        scales[t] = lax.rsqrt(pivots)
+        x[t] = kept * scales[t]
     return x, scales
 
 
@@ -206,7 +219,7 @@
     n_rep = len(pieces)
     docs = p_ref.shape[0]
     rows = docs // n_rep
-    tokens = p_ref.shape[1]
+    tokens = p_ref.shape[1] // 4
     me = me_ref[0]
     for d in range(n_rep):
         tok_ref[me ^ d] = pieces[d][...]
@@ -214,27 +227,35 @@
     len_ref[...] = jnp.zeros_like(len_ref)
     side = (tok_ref.shape[1] - 16) // 2
     doc = lax.broadcasted_iota(jnp.int32, (docs, tokens), 0).astype(jnp.float32)
-    ones = jnp.ones((16, tokens), jnp.bfloat16)
+    ones = jnp.ones((16, 2 * tokens), jnp.bfloat16)
     tall = 8 * side
 
-    def add_tokens(r, last):
-        left = tok_ref[r, 0:side, :].astype(jnp.float32)
-        right = tok_ref[r, side : 2 * side, :].astype(jnp.float32)
-        coded = tok_ref[r, 2 * side :, :].astype(jnp.float32)
-        target = coded[0:1, :] * 32.0 + coded[1:2, :]
-        target = jnp.where(target < 0.0, last, target)
-        p_ref[...] = jnp.where(doc == target, 1.0, 0.0).astype(jnp.bfloat16)
-        len_ref[...] += dot_n(ones, p_ref[...])
+    def add_tokens(pair, last):
+        for h in range(2):
+            coded = tok_ref[2 * pair + h, 2 * side :, :].astype(jnp.float32)
+            target = coded[0:1, :] * 32.0 + coded[1:2, :]
+            target = jnp.where(target < 0.0, last, target)
+            last = target[:, tokens - 1 : tokens]
+            member = jnp.where(doc == target, 1.0, 0.0).astype(jnp.bfloat16)
+            p_ref[:, h * tokens : (h + 1) * tokens] = member
+            p_ref[:, (h + 2) * tokens : (h + 3) * tokens] = member
+        len_ref[...] += dot_n(ones, p_ref[:, 0 : 2 * tokens])
+        lefts = [tok_ref[2 * pair + h, 0:side, :].astype(jnp.float32) for h in range(2)]
+        rights = [tok_ref[2 * pair + h, side : 2 * side, :].astype(jnp.float32) for h in range(2)]
         for q in range(0, side, 8):
-            outer = jnp.concatenate(
-                [jnp.broadcast_to(left[i : i + 1, :], right.shape) * right for i in range(q, q + 8)], 0
-            )
-            high = outer.astype(jnp.bfloat16)
-            low = (outer - high.astype(jnp.float32)).astype(jnp.bfloat16)
-            sum_ref[q * side : q * side + tall, :] += dot_n(high, p_ref[...]) + dot_n(low, p_ref[...])
-        return target[:, tokens - 1 : tokens]
-
-    lax.fori_loop(0, n_rep, add_tokens, jnp.zeros((1, 1), jnp.float32))
+            highs, lows = [], []
+            for h in range(2):
+                left, right = lefts[h], rights[h]
+                outer = jnp.concatenate(
+                    [jnp.broadcast_to(left[i : i + 1, :], right.shape) * right for i in range(q, q + 8)], 0
+                )
+                highs.append(outer.astype(jnp.bfloat16))
+                lows.append((outer - highs[h].astype(jnp.float32)).astype(jnp.bfloat16))
+            parts = jnp.concatenate(highs + lows, 1)
+            sum_ref[q * side : q * side + tall, :] += dot_n(parts, p_ref[...])
+        return last
+
+    lax.fori_loop(0, n_rep // 2, add_tokens, jnp.zeros((1, 1), jnp.float32))
     scale = lax.rsqrt(jnp.maximum(len_ref[0:1, :], 1.0))
     f_ref[...] = (sum_ref[...] * scale).astype(jnp.bfloat16)
     row = lax.broadcasted_iota(jnp.int32, (docs, BLK), 0)
@@ -324,7 +345,7 @@
             pltpu.VMEM((n_rep, height, tokens), jnp.bfloat16),
             pltpu.VMEM((width, docs), jnp.float32),
             pltpu.VMEM((16, docs), jnp.float32),
-            pltpu.VMEM((docs, tokens), jnp.bfloat16),
+            pltpu.VMEM((docs, 4 * tokens), jnp.bfloat16),
             pltpu.VMEM((width, docs), jnp.bfloat16),
             pltpu.VMEM((width, width + BLK), jnp.float32),
             pltpu.VMEM((PAN, width + BLK), jnp.float32),

time: 77 us -> 69 us (0.90)
  Pallas kernels: 52.9 us -> 44.9 us
    pallas_call x1, Pallas kernels: 45.2 us -> 37.2 us  [factor_and_solve(): pl.pallas_call(functools.partial(factor_kernel, width), out_shape=[jax.Sh...]
where the time goes in v2:
time: 69 us; the launch traced here: 68.8 us
  Pallas kernels  44.9 us (65%)
  starting transfers between devices  13.1 us (19%)
  waiting for transfers between devices  8.7 us (13%)
  local copies, waits for them, and re-layouts  1.4 us (2%)
    pallas_call x1, Pallas kernels, factor_and_solve(): pl.pallas_call(functools.partial(factor_kernel, width), out_shape=[jax.Sh...  37.2 us
    ppermute x10, starting transfers between devices, swapped(): return lax.ppermute(block, axis, [(i, i ^ distance) for i in devices])  13.1 us
    ppermute x10, waiting for transfers between devices, swapped(): return lax.ppermute(block, axis, [(i, i ^ distance) for i in devices])  8.7 us
    pallas_call x1, Pallas kernels, project(): pl.pallas_call(project_kernel, out_shape=jax.ShapeDtypeStruct((2 * width...  7.7 us
  transfers between devices with their start and end apart: 10, of which 6 were waited for; matrix products, arithmetic and copies ran while one was open for 0% of the time, Pallas kernels for 0%

profile of v2, /device:TPU:0, one launch (start us, length us, event | category | flops | bytes accessed | tf_op | source)
XLA Modules:
  0.0 68.8 jit_solution(4180594289723438288)
XLA Ops:
  0.6 7.7 %project.1.refs_0_ = bf16[80,512]{1,0:T(8,128)(2,1)} custom-call(bf16[512,8192]{1,0:T(8,128)(2,1)} %bitcast.11, bf16[512,8192]{1,0:T(8,128)(2,1)} %bitcast.12, bf16[32,8192]{1,0:T(8,128)(2,1)} %bitcast.13, bf16[32,8192]{1,0:T(8,128)(2,1)} %bitcast.14, s32[1,512]{1,0:T(1,128)} %bitcast.15, s32[1,62]{1,0:T(1,128)} %bitcast.16), custom_call_target="tpu_custom_call" | custom-call | tf_op jit(solution)/shard_map/project/pallas_call | solution.py:108
  8.3 5.1 %collective-permute-start.5 = (bf16[80,512]{1,0:T(8,128)(2,1)}, bf16[80,512]{1,0:T(8,128)(2,1)S(1)}, u32[]{:S(2)}, u32[]{:S(2)}) collective-permute-start(bf16[80,512]{1,0:T(8,128)(2,1)} %project.1.refs_0_), channel_id=1, source_target_pairs={{0,24},{4,28},{8,16},{12,20},{16,8},{20,12},{24,0},{28,4},{1,25},{... | collective-permute-start | bytes 245768 | tf_op jit(solution)/shard_map/ppermute | solution.py:22
  13.4 0.0 collective-permute-start.3
  13.4 0.6 collective-permute-start.1
  14.1 1.6 %collective-permute-start = (bf16[80,512]{1,0:T(8,128)(2,1)}, bf16[80,512]{1,0:T(8,128)(2,1)S(1)}, u32[]{:S(2)}, u32[]{:S(2)}) collective-permute-start(bf16[80,512]{1,0:T(8,128)(2,1)} %project.1.refs_0_), channel_id=1, source_target_pairs={{0,4},{4,0},{8,12},{12,8},{16,20},{20,16},{24,28},{28,24},{1,5},{5... | collective-permute-start | bytes 245768 | tf_op jit(solution)/shard_map/ppermute | solution.py:22
  15.7 1.0 %collective-permute-done.5.refs_6_ = bf16[80,512]{1,0:T(8,128)(2,1)S(1)} collective-permute-done((bf16[80,512]{1,0:T(8,128)(2,1)}, bf16[80,512]{1,0:T(8,128)(2,1)S(1)}, u32[]{:S(2)}, u32[]{:S(2)}) %collective-permute-start.5) | collective-permute-done | bytes 81952 | tf_op jit(solution)/shard_map/ppermute | solution.py:22
  16.7 1.8 %collective-permute-start.6 = (bf16[80,512]{1,0:T(8,128)(2,1)S(1)}, bf16[80,512]{1,0:T(8,128)(2,1)S(1)}, u32[]{:S(2)}, u32[]{:S(2)}) collective-permute-start(bf16[80,512]{1,0:T(8,128)(2,1)S(1)} %collective-permute-done.5.refs_6_), channel_id=1, source_target_pairs={{0,4},{4,0},{8,12},{12,8},{16,20},{20,16},{24,28},{28,24},{1,5},{5... | collective-permute-start | bytes 245768 | tf_op jit(solution)/shard_map/ppermute | solution.py:22
  18.4 2.1 %collective-permute-done.3.refs_4_ = bf16[80,512]{1,0:T(8,128)(2,1)S(1)} collective-permute-done((bf16[80,512]{1,0:T(8,128)(2,1)}, bf16[80,512]{1,0:T(8,128)(2,1)S(1)}, u32[]{:S(2)}, u32[]{:S(2)}) %collective-permute-start.3) | collective-permute-done | bytes 81952 | tf_op jit(solution)/shard_map/ppermute | solution.py:22
  20.5 1.5 %collective-permute-start.4 = (bf16[80,512]{1,0:T(8,128)(2,1)S(1)}, bf16[80,512]{1,0:T(8,128)(2,1)S(1)}, u32[]{:S(2)}, u32[]{:S(2)}) collective-permute-start(bf16[80,512]{1,0:T(8,128)(2,1)S(1)} %collective-permute-done.3.refs_4_), channel_id=1, source_target_pairs={{0,4},{4,0},{8,12},{12,8},{16,20},{20,16},{24,28},{28,24},{1,5},{5... | collective-permute-start | bytes 245768 | tf_op jit(solution)/shard_map/ppermute | solution.py:22
  22.0 0.0 collective-permute-done.1.refs_2_
  22.0 0.5 collective-permute-start.2
  22.5 0.0 collective-permute-done.refs_1_
  22.6 0.0 collective-permute-done.6.refs_7_
  22.6 3.0 %collective-permute-done.4.refs_5_ = bf16[80,512]{1,0:T(8,128)(2,1)S(1)} collective-permute-done((bf16[80,512]{1,0:T(8,128)(2,1)S(1)}, bf16[80,512]{1,0:T(8,128)(2,1)S(1)}, u32[]{:S(2)}, u32[]{:S(2)}) %collective-permute-start.4) | collective-permute-done | bytes 81952 | tf_op jit(solution)/shard_map/ppermute | solution.py:22
  25.5 0.9 %collective-permute-done.2.refs_3_ = bf16[80,512]{1,0:T(8,128)(2,1)S(1)} collective-permute-done((bf16[80,512]{1,0:T(8,128)(2,1)S(1)}, bf16[80,512]{1,0:T(8,128)(2,1)S(1)}, u32[]{:S(2)}, u32[]{:S(2)}) %collective-permute-start.2) | collective-permute-done | bytes 81952 | tf_op jit(solution)/shard_map/ppermute | solution.py:22
  26.5 0.0 copy-start
  26.5 0.9 %copy-done = bf16[80,512]{1,0:T(8,128)(2,1)S(1)} copy-done((bf16[80,512]{1,0:T(8,128)(2,1)S(1)}, bf16[80,512]{1,0:T(8,128)(2,1)}, u32[]{:S(2)}) %copy-start) | copy-done | bytes 81944
  27.3 37.2 %factor.1 = (f32[1024,1024]{1,0:T(8,128)}, bf16[32,1024]{1,0:T(8,128)(2,1)}, f32[1,128]{1,0:T(1,128)S(1)}) custom-call(s32[1]{0:T(128)} %bitcast.me_ref, bf16[80,512]{1,0:T(8,128)(2,1)S(1)} %copy-done, bf16[80,512]{1,0:T(8,128)(2,1)S(1)} %collective-permute-done.refs_1_, bf16[80,512]{1,0:T(8,128)(2,1)S(1)} %collective-permute-done.1.refs_2_, ...), custom_call_target="tpu_custom_call" | custom-call | tf_op jit(solution)/shard_map/factor/pallas_call | solution.py:335
  64.6 0.1 collective-permute-start.9
  64.7 1.6 %collective-permute-start.8 = (f32[1,128]{1,0:T(1,128)S(1)}, f32[1,128]{1,0:T(1,128)S(1)}, u32[]{:S(2)}, u32[]{:S(2)}) collective-permute-start(f32[1,128]{1,0:T(1,128)S(1)} %get-tuple-element.8), channel_id=1, source_target_pairs={{0,2},{1,3},{2,0},{3,1},{4,6},{5,7},{6,4},{7,5},{8,10},{9,11},{10,... | collective-permute-start | bytes 1544 | tf_op jit(solution)/shard_map/ppermute | solution.py:22
  66.2 0.3 collective-permute-start.7
  66.5 1.1 %collective-permute-done.9 = f32[1,128]{1,0:T(1,128)S(1)} collective-permute-done((f32[1,128]{1,0:T(1,128)S(1)}, f32[1,128]{1,0:T(1,128)S(1)}, u32[]{:S(2)}, u32[]{:S(2)}) %collective-permute-start.9) | collective-permute-done | bytes 544 | tf_op jit(solution)/shard_map/ppermute | solution.py:22
  67.6 0.7 collective-permute-done.8
  68.3 0.0 collective-permute-done.7
  68.3 0.5 slice_bitcast_fusion
  (1 shorter events, 0.0 us)
Async XLA Ops:
  8.3 8.3 %collective-permute-start.5 = (bf16[80,512]{1,0:T(8,128)(2,1)}, bf16[80,512]{1,0:T(8,128)(2,1)S(1)}, u32[]{:S(2)}, u32[]{:S(2)}) collective-permute-start(bf16[80,512]{1,0:T(8,128)(2,1)} %project.1.refs_0_), channel_id=1, source_target_pairs={{0,24},{4,28},{8,16},{12,20},{16,8},{20,12},{24,0},{28,4},{1,25},{... | collective-permute-start | bytes 245768 | tf_op jit(solution)/shard_map/ppermute | solution.py:22
  13.4 7.1 %collective-permute-start.3 = (bf16[80,512]{1,0:T(8,128)(2,1)}, bf16[80,512]{1,0:T(8,128)(2,1)S(1)}, u32[]{:S(2)}, u32[]{:S(2)}) collective-permute-start(bf16[80,512]{1,0:T(8,128)(2,1)} %project.1.refs_0_), channel_id=1, source_target_pairs={{0,16},{4,20},{8,24},{12,28},{16,0},{20,4},{24,8},{28,12},{1,17},{... | collective-permute-start | bytes 245768 | tf_op jit(solution)/shard_map/ppermute | solution.py:22
  13.4 8.6 %collective-permute-start.1 = (bf16[80,512]{1,0:T(8,128)(2,1)}, bf16[80,512]{1,0:T(8,128)(2,1)S(1)}, u32[]{:S(2)}, u32[]{:S(2)}) collective-permute-start(bf16[80,512]{1,0:T(8,128)(2,1)} %project.1.refs_0_), channel_id=1, source_target_pairs={{0,8},{4,12},{8,0},{12,4},{16,24},{20,28},{24,16},{28,20},{1,9},{5... | collective-permute-start | bytes 245768 | tf_op jit(solution)/shard_map/ppermute | solution.py:22
  14.1 8.5 %collective-permute-start = (bf16[80,512]{1,0:T(8,128)(2,1)}, bf16[80,512]{1,0:T(8,128)(2,1)S(1)}, u32[]{:S(2)}, u32[]{:S(2)}) collective-permute-start(bf16[80,512]{1,0:T(8,128)(2,1)} %project.1.refs_0_), channel_id=1, source_target_pairs={{0,4},{4,0},{8,12},{12,8},{16,20},{20,16},{24,28},{28,24},{1,5},{5... | collective-permute-start | bytes 245768 | tf_op jit(solution)/shard_map/ppermute | solution.py:22
  16.7 5.9 %collective-permute-start.6 = (bf16[80,512]{1,0:T(8,128)(2,1)S(1)}, bf16[80,512]{1,0:T(8,128)(2,1)S(1)}, u32[]{:S(2)}, u32[]{:S(2)}) collective-permute-start(bf16[80,512]{1,0:T(8,128)(2,1)S(1)} %collective-permute-done.5.refs_6_), channel_id=1, source_target_pairs={{0,4},{4,0},{8,12},{12,8},{16,20},{20,16},{24,28},{28,24},{1,5},{5... | collective-permute-start | bytes 245768 | tf_op jit(solution)/shard_map/ppermute | solution.py:22
  20.5 5.0 %collective-permute-start.4 = (bf16[80,512]{1,0:T(8,128)(2,1)S(1)}, bf16[80,512]{1,0:T(8,128)(2,1)S(1)}, u32[]{:S(2)}, u32[]{:S(2)}) collective-permute-start(bf16[80,512]{1,0:T(8,128)(2,1)S(1)} %collective-permute-done.3.refs_4_), channel_id=1, source_target_pairs={{0,4},{4,0},{8,12},{12,8},{16,20},{20,16},{24,28},{28,24},{1,5},{5... | collective-permute-start | bytes 245768 | tf_op jit(solution)/shard_map/ppermute | solution.py:22
  22.0 4.4 %collective-permute-start.2 = (bf16[80,512]{1,0:T(8,128)(2,1)S(1)}, bf16[80,512]{1,0:T(8,128)(2,1)S(1)}, u32[]{:S(2)}, u32[]{:S(2)}) collective-permute-start(bf16[80,512]{1,0:T(8,128)(2,1)S(1)} %collective-permute-done.1.refs_2_), channel_id=1, source_target_pairs={{0,4},{4,0},{8,12},{12,8},{16,20},{20,16},{24,28},{28,24},{1,5},{5... | collective-permute-start | bytes 245768 | tf_op jit(solution)/shard_map/ppermute | solution.py:22
  26.5 0.9 %copy-start = (bf16[80,512]{1,0:T(8,128)(2,1)S(1)}, bf16[80,512]{1,0:T(8,128)(2,1)}, u32[]{:S(2)}) copy-start(bf16[80,512]{1,0:T(8,128)(2,1)} %project.1.refs_0_) | copy-start | bytes 245764
  64.6 3.0 %collective-permute-start.9 = (f32[1,128]{1,0:T(1,128)S(1)}, f32[1,128]{1,0:T(1,128)S(1)}, u32[]{:S(2)}, u32[]{:S(2)}) collective-permute-start(f32[1,128]{1,0:T(1,128)S(1)} %get-tuple-element.8), channel_id=1, source_target_pairs={{0,3},{1,2},{2,1},{3,0},{4,7},{5,6},{6,5},{7,4},{8,11},{9,10},{10,... | collective-permute-start | bytes 1544 | tf_op jit(solution)/shard_map/ppermute | solution.py:22
  64.7 3.6 %collective-permute-start.8 = (f32[1,128]{1,0:T(1,128)S(1)}, f32[1,128]{1,0:T(1,128)S(1)}, u32[]{:S(2)}, u32[]{:S(2)}) collective-permute-start(f32[1,128]{1,0:T(1,128)S(1)} %get-tuple-element.8), channel_id=1, source_target_pairs={{0,2},{1,3},{2,0},{3,1},{4,6},{5,7},{6,4},{7,5},{8,10},{9,11},{10,... | collective-permute-start | bytes 1544 | tf_op jit(solution)/shard_map/ppermute | solution.py:22
  66.2 2.0 %collective-permute-start.7 = (f32[1,128]{1,0:T(1,128)S(1)}, f32[1,128]{1,0:T(1,128)S(1)}, u32[]{:S(2)}, u32[]{:S(2)}) collective-permute-start(f32[1,128]{1,0:T(1,128)S(1)} %get-tuple-element.8), channel_id=1, source_target_pairs={{0,1},{1,0},{2,3},{3,2},{4,5},{5,4},{6,7},{7,6},{8,9},{9,8},{10,11... | collective-permute-start | bytes 1544 | tf_op jit(solution)/shard_map/ppermute | solution.py:22

commit v3 on v2

--- a/solution.py
+++ b/solution.py
@@ -38,14 +38,24 @@
     return jnp.broadcast_to(v[s : s + 1, :], v.shape)
 
 
-def dot(a, b, precision=EXACT):
-    return jnp.dot(a, b, precision=precision, preferred_element_type=jnp.float32)
-
-
-def dot_t(a, b, precision=EXACT):
+def dot_t(a, b):
     return lax.dot_general(
-        a, b, (((0,), (0,)), ((), ())), precision=precision, preferred_element_type=jnp.float32
-    )
+        a, b, (((0,), (0,)), ((), ())), precision=EXACT, preferred_element_type=jnp.float32
+    )
+
+
+def split(x):
+    high = x.astype(jnp.bfloat16)
+    rest = x - high.astype(jnp.float32)
+    middle = rest.astype(jnp.bfloat16)
+    return high, middle, (rest - middle.astype(jnp.float32)).astype(jnp.bfloat16)
+
+
+def dot_parts(a, b, dim_a, dim_b=0):
+    left = jnp.concatenate([a[2], a[1], a[0], a[1], a[0], a[0]], dim_a)
+    right = jnp.concatenate([b[0], b[1], b[2], b[0], b[1], b[0]], dim_b)
+    dims = (((dim_a,), (dim_b,)), ((), ()))
+    return lax.dot_general(left, right, dims, preferred_element_type=jnp.float32)
 
 
 def dot_n(a, b):
@@ -138,42 +148,40 @@
     scales = [None] * count
     spread = lambda group, lo: [lane_of(group, lo + c) for c in range(8)]
     cols = spread(x[0], first)
+    pivot = row_of(cols[0], 0)
     for t in range(count):
         lo = first + 8 * t
         work = x[t]
         more = t + 1 < count
         if more:
             below = [spread(x[i], lo) for i in range(t + 1, count)]
-            side = spread(x[t], lo + 8)
             ahead = spread(x[t + 1], lo + 8)
             factor = list(below[0])
         kept, pivots = work, jnp.ones((8, BLK), jnp.float32)
         for c in range(8):
             hit, at = sub == c, lane == lo + c
-            pivot = row_of(cols[c], c)
             inv = 1.0 / pivot
             kept = jnp.where(hit, work, kept)
             pivots = jnp.where(hit, pivot, pivots)
-            row = jnp.where(at, 1.0, row_of(work, c)) * inv
-            work = jnp.where(hit, row, jnp.where(at, 0.0, work) - cols[c] * row)
-            under = jnp.where(sub > c, cols[c], 0.0)
+            other = jnp.where(hit, 0.0, cols[c])
+            scaled = other * inv
+            raws = {k: row_of(cols[c], k) for k in range(c + 1, 8)}
+            if c < 7:
+                pivot = row_of(cols[c + 1], c + 1) - (raws[c + 1] * raws[c + 1]) * inv
+            elif more:
+                edge = row_of(factor[7], 0)
+                pivot = row_of(ahead[0], 0) - (edge * edge) * inv
+            row = jnp.where(at, 1.0, row_of(work, c))
+            work = jnp.where(at, jnp.where(hit, 1.0, 0.0), work) - scaled * row
             for k in range(c + 1, 8):
-                raw = row_of(cols[k], c)
-                weight = raw * inv
-                if k == c + 1:
-                    new = cols[k] - (cols[c] * raw) * inv
-                else:
-                    new = cols[k] - cols[c] * weight
-                cols[k] = jnp.where(hit, weight, new)
-                if more:
-                    factor[k] = factor[k] - factor[c] * weight
+                cols[k] = cols[k] - scaled * raws[k]
             if more:
+                part = factor[c] * inv
+                for k in range(c + 1, 8):
+                    factor[k] = factor[k] - part * raws[k]
                 for k in range(8):
-                    raw = row_of(side[k], c)
-                    weight = raw * inv
-                    if c < 7:
-                        side[k] = side[k] - under * weight
-                    ahead[k] = ahead[k] - factor[c] * weight
+                    ahead[k] = ahead[k] - part * row_of(factor[c], k)
+        work = work * (1.0 / pivots)
         if more:
             inside = (lane >= lo) & (lane < lo + 8)
             rows = [row_of(work, c) for c in range(8)]
@@ -215,7 +223,7 @@
 
 
 def factor_kernel(width, me_ref, *refs):
-    *pieces, u_out, mine_out, quad_ref, tok_ref, sum_ref, len_ref, p_ref, f_ref, u_ref, s_ref, d_ref, m_ref, sems = refs
+    *pieces, u_out, mine_out, quad_ref, tok_ref, sum_ref, len_ref, p_ref, f_ref, u_ref, u3_ref, s_ref, y_ref, own_ref, d_ref, m_ref, sems = refs
     n_rep = len(pieces)
     docs = p_ref.shape[0]
     rows = docs // n_rep
@@ -258,9 +266,6 @@
     lax.fori_loop(0, n_rep // 2, add_tokens, jnp.zeros((1, 1), jnp.float32))
     scale = lax.rsqrt(jnp.maximum(len_ref[0:1, :], 1.0))
     f_ref[...] = (sum_ref[...] * scale).astype(jnp.bfloat16)
-    row = lax.broadcasted_iota(jnp.int32, (docs, BLK), 0)
-    slot = lax.broadcasted_iota(jnp.int32, (docs, BLK), 1)
-    pick = jnp.where((row == me * rows + slot) & (slot < rows), 1.0, 0.0).astype(jnp.bfloat16)
     row = lax.broadcasted_iota(jnp.int32, (rows, docs), 0)
     slot = lax.broadcasted_iota(jnp.int32, (rows, docs), 1)
     pick_t = jnp.where(slot == me * rows + row, 1.0, 0.0).astype(jnp.bfloat16)
@@ -273,36 +278,48 @@
 
     def start_panel(k):
         a, c = PAN * k, PAN * k + PAN
-        gram = dot_n(f_ref[a:c, :], f_ref[a:, :]) * (1.0 / docs)
-        own = dot(f_ref[a:c, :], pick, None)
+        s_ref[:, a:] = dot_n(f_ref[a:c, :], f_ref[a:, :]) * (1.0 / docs)
+        s_ref[:, a:c] = s_ref[:, a:c] + eye
+        own = mine_out[:, a:c].astype(jnp.float32)
         if k:
-            done = u_ref[0:a, a:c]
-            gram = gram - dot_t(done, u_ref[0:a, a:width])
-            own = own - dot_t(done, u_ref[0:a, width:])
+            done = [u3_ref[p, 0:a, a:c] for p in range(3)]
+            s_ref[:, a:] = s_ref[:, a:] - dot_parts(done, [u3_ref[p, 0:a, a:] for p in range(3)], 0)
+            own = own - dot_parts(split(y_ref[:, 0:a]), done, 1)
             u_ref[a:c, 0:a] = jnp.zeros((PAN, a), jnp.float32)
+        own_ref[...] = own
         u_ref[a + BLK : c, a : a + BLK] = jnp.zeros((BLK, BLK), jnp.float32)
-        s_ref[:, a:c] = gram[:, 0:PAN] + eye
-        if c < width:
-            s_ref[:, c:width] = gram[:, PAN:]
-        s_ref[:, width:] = own
         d_ref[...] = s_ref[0:BLK, a : a + BLK]
+
+    def keep(rows, at, value):
+        u_ref[rows, at] = value
+        parts = split(value)
+        for p in range(3):
+            u3_ref[p, rows, at] = parts[p]
+        return parts
+
+    def block_copy(m):
+        at = pl.ds(BLK * m, BLK)
+        return pltpu.make_async_copy(u_ref.at[at, :], u_out.at[at, :], sems.at[m])
 
     def first_half(k):
         a, b, c = PAN * k, PAN * k + BLK, PAN * k + PAN
-        upper = dot(m_ref[...], s_ref[0:BLK, b:])
-        u_ref[a:b, b:] = upper
-        update = dot_t(upper[:, 0:BLK], upper)
-        d_ref[...] = s_ref[BLK:, b:c] - update[:, 0:BLK]
-        s_ref[BLK:, c:] = s_ref[BLK:, c:] - update[:, BLK:]
-
-    def panel_copy(k):
-        at = pl.ds(PAN * k, PAN)
-        return pltpu.make_async_copy(u_ref.at[at, 0:width], u_out.at[at, :], sems.at[k])
+        inverse = split(m_ref[...])
+        upper = keep(slice(a, b), slice(b, None), dot_parts(inverse, split(s_ref[0:BLK, b:]), 1))
+        corner = [part[:, 0:BLK] for part in upper]
+        s_ref[BLK:, b:] = s_ref[BLK:, b:] - dot_parts(corner, upper, 0)
+        d_ref[...] = s_ref[BLK:, b:c]
+        block_copy(2 * k).start()
+        solved = dot_parts(split(own_ref[:, 0:BLK]), inverse, 1, 1)
+        y_ref[:, a:b] = solved
+        own_ref[:, BLK:] = own_ref[:, BLK:] - dot_parts(split(solved), corner, 1)
 
     def second_half(k):
         b, c = PAN * k + BLK, PAN * k + PAN
-        u_ref[b:c, c:] = dot(m_ref[...], s_ref[BLK:, c:])
-        panel_copy(k).start()
+        inverse = split(m_ref[...])
+        if c < width:
+            keep(slice(b, c), slice(c, None), dot_parts(inverse, split(s_ref[BLK:, c:]), 1))
+        block_copy(2 * k + 1).start()
+        y_ref[:, b:c] = dot_parts(split(own_ref[:, BLK:]), inverse, 1, 1)
         if c < width:
             start_panel(k + 1)
 
@@ -320,11 +337,11 @@
         return carry
 
     lax.fori_loop(0, width // BLK, block, 0)
-    solved = u_ref[:, width:]
-    quad = jnp.sum(solved * solved, axis=0, keepdims=True) * (1.0 / width)
-    quad_ref[...] = quad
-    for k in range(width // PAN):
-        panel_copy(k).wait()
+    squares = y_ref[...] * y_ref[...]
+    quad = sum(squares[:, c : c + BLK] for c in range(0, width, BLK))
+    quad_ref[...] = jnp.sum(quad.T, axis=0, keepdims=True) * (1.0 / width)
+    for m in range(width // BLK):
+        block_copy(m).wait()
 
 
 def factor_and_solve(pieces, replica):
@@ -337,7 +354,7 @@
         out_shape=[
             jax.ShapeDtypeStruct((width, width), jnp.float32),
             jax.ShapeDtypeStruct((BAL, width), jnp.bfloat16),
-            jax.ShapeDtypeStruct((1, BLK), jnp.float32),
+            jax.ShapeDtypeStruct((1, BAL), jnp.float32),
         ],
         in_specs=[pl.BlockSpec(memory_space=pltpu.SMEM)] + [VMEM] * n_rep,
         out_specs=[pl.BlockSpec(memory_space=pl.ANY), VMEM, VMEM],
@@ -347,11 +364,14 @@
             pltpu.VMEM((16, docs), jnp.float32),
             pltpu.VMEM((docs, 4 * tokens), jnp.bfloat16),
             pltpu.VMEM((width, docs), jnp.bfloat16),
-            pltpu.VMEM((width, width + BLK), jnp.float32),
-            pltpu.VMEM((PAN, width + BLK), jnp.float32),
+            pltpu.VMEM((width, width), jnp.float32),
+            pltpu.VMEM((3, width, width), jnp.bfloat16),
+            pltpu.VMEM((PAN, width), jnp.float32),
+            pltpu.VMEM((BAL, width), jnp.float32),
+            pltpu.VMEM((BAL, PAN), jnp.float32),
             pltpu.VMEM((BLK, BLK), jnp.float32),
             pltpu.VMEM((BLK, BLK), jnp.float32),
-            pltpu.SemaphoreType.DMA((width // PAN,)),
+            pltpu.SemaphoreType.DMA((width // BLK,)),
         ],
         compiler_params=pltpu.CompilerParams(vmem_limit_bytes=48 * 1024 * 1024),
         name="factor",
@@ -366,7 +386,7 @@
     layers = [quad] + [swapped(quad, "layer", d) for d in range(1, lax.axis_size("layer"))]
     while len(layers) > 1:
         layers = [layers[i] + layers[i + 1] for i in range(0, len(layers), 2)]
-    return (upper[None], mine[None], layers[0][0, :BAL])
+    return (upper[None], mine[None], layers[0][0])
 
 
 def solution(mesh):

time: 69 us -> 64.5 us (0.935)
  Pallas kernels: 44.9 us -> 40.5 us
    pallas_call x1, Pallas kernels: 37.2 us -> 32.8 us  [factor_and_solve(): pl.pallas_call(functools.partial(factor_kernel, width), out_shape=[jax.Sh...]
where the time goes in v3:
time: 64.5 us; the launch traced here: 64.3 us
  Pallas kernels  40.5 us (63%)
  starting transfers between devices  13.1 us (20%)
  waiting for transfers between devices  8.7 us (13%)
  local copies, waits for them, and re-layouts  0.89 us (1%)
  between operations  0.67 us (1%)
    pallas_call x1, Pallas kernels, factor_and_solve(): pl.pallas_call(functools.partial(factor_kernel, width), out_shape=[jax.Sh...  32.8 us
    ppermute x10, starting transfers between devices, swapped(): return lax.ppermute(block, axis, [(i, i ^ distance) for i in devices])  13.1 us
    ppermute x10, waiting for transfers between devices, swapped(): return lax.ppermute(block, axis, [(i, i ^ distance) for i in devices])  8.7 us
    pallas_call x1, Pallas kernels, project(): pl.pallas_call(project_kernel, out_shape=jax.ShapeDtypeStruct((2 * width...  7.7 us
  transfers between devices with their start and end apart: 10, of which 6 were waited for; matrix products, arithmetic and copies ran while one was open for 0% of the time, Pallas kernels for 0%

profile of v3, /device:TPU:0, one launch (start us, length us, event | category | flops | bytes accessed | tf_op | source)
XLA Modules:
  0.0 64.3 jit_solution(11681835428961531401)
XLA Ops:
  0.6 7.7 %project.1.refs_0_ = bf16[80,512]{1,0:T(8,128)(2,1)} custom-call(bf16[512,8192]{1,0:T(8,128)(2,1)} %bitcast.11, bf16[512,8192]{1,0:T(8,128)(2,1)} %bitcast.12, bf16[32,8192]{1,0:T(8,128)(2,1)} %bitcast.13, bf16[32,8192]{1,0:T(8,128)(2,1)} %bitcast.14, s32[1,512]{1,0:T(1,128)} %bitcast.15, s32[1,62]{1,0:T(1,128)} %bitcast.16), custom_call_target="tpu_custom_call" | custom-call | tf_op jit(solution)/shard_map/project/pallas_call | solution.py:118
  8.3 5.1 %collective-permute-start.5 = (bf16[80,512]{1,0:T(8,128)(2,1)}, bf16[80,512]{1,0:T(8,128)(2,1)S(1)}, u32[]{:S(2)}, u32[]{:S(2)}) collective-permute-start(bf16[80,512]{1,0:T(8,128)(2,1)} %project.1.refs_0_), channel_id=1, source_target_pairs={{0,24},{4,28},{8,16},{12,20},{16,8},{20,12},{24,0},{28,4},{1,25},{... | collective-permute-start | bytes 245768 | tf_op jit(solution)/shard_map/ppermute | solution.py:22
  13.4 0.0 collective-permute-start.3
  13.4 0.6 collective-permute-start.1
  14.1 1.6 %collective-permute-start = (bf16[80,512]{1,0:T(8,128)(2,1)}, bf16[80,512]{1,0:T(8,128)(2,1)S(1)}, u32[]{:S(2)}, u32[]{:S(2)}) collective-permute-start(bf16[80,512]{1,0:T(8,128)(2,1)} %project.1.refs_0_), channel_id=1, source_target_pairs={{0,4},{4,0},{8,12},{12,8},{16,20},{20,16},{24,28},{28,24},{1,5},{5... | collective-permute-start | bytes 245768 | tf_op jit(solution)/shard_map/ppermute | solution.py:22
  15.7 1.0 %collective-permute-done.5.refs_6_ = bf16[80,512]{1,0:T(8,128)(2,1)S(1)} collective-permute-done((bf16[80,512]{1,0:T(8,128)(2,1)}, bf16[80,512]{1,0:T(8,128)(2,1)S(1)}, u32[]{:S(2)}, u32[]{:S(2)}) %collective-permute-start.5) | collective-permute-done | bytes 81952 | tf_op jit(solution)/shard_map/ppermute | solution.py:22
  16.7 1.8 %collective-permute-start.6 = (bf16[80,512]{1,0:T(8,128)(2,1)S(1)}, bf16[80,512]{1,0:T(8,128)(2,1)S(1)}, u32[]{:S(2)}, u32[]{:S(2)}) collective-permute-start(bf16[80,512]{1,0:T(8,128)(2,1)S(1)} %collective-permute-done.5.refs_6_), channel_id=1, source_target_pairs={{0,4},{4,0},{8,12},{12,8},{16,20},{20,16},{24,28},{28,24},{1,5},{5... | collective-permute-start | bytes 245768 | tf_op jit(solution)/shard_map/ppermute | solution.py:22
  18.4 2.1 %collective-permute-done.3.refs_4_ = bf16[80,512]{1,0:T(8,128)(2,1)S(1)} collective-permute-done((bf16[80,512]{1,0:T(8,128)(2,1)}, bf16[80,512]{1,0:T(8,128)(2,1)S(1)}, u32[]{:S(2)}, u32[]{:S(2)}) %collective-permute-start.3) | collective-permute-done | bytes 81952 | tf_op jit(solution)/shard_map/ppermute | solution.py:22
  20.5 1.5 %collective-permute-start.4 = (bf16[80,512]{1,0:T(8,128)(2,1)S(1)}, bf16[80,512]{1,0:T(8,128)(2,1)S(1)}, u32[]{:S(2)}, u32[]{:S(2)}) collective-permute-start(bf16[80,512]{1,0:T(8,128)(2,1)S(1)} %collective-permute-done.3.refs_4_), channel_id=1, source_target_pairs={{0,4},{4,0},{8,12},{12,8},{16,20},{20,16},{24,28},{28,24},{1,5},{5... | collective-permute-start | bytes 245768 | tf_op jit(solution)/shard_map/ppermute | solution.py:22
  22.0 0.0 collective-permute-done.1.refs_2_
  22.0 0.5 collective-permute-start.2
  22.5 0.0 collective-permute-done.refs_1_
  22.6 0.0 collective-permute-done.6.refs_7_
  22.6 3.0 %collective-permute-done.4.refs_5_ = bf16[80,512]{1,0:T(8,128)(2,1)S(1)} collective-permute-done((bf16[80,512]{1,0:T(8,128)(2,1)S(1)}, bf16[80,512]{1,0:T(8,128)(2,1)S(1)}, u32[]{:S(2)}, u32[]{:S(2)}) %collective-permute-start.4) | collective-permute-done | bytes 81952 | tf_op jit(solution)/shard_map/ppermute | solution.py:22
  25.5 0.9 %collective-permute-done.2.refs_3_ = bf16[80,512]{1,0:T(8,128)(2,1)S(1)} collective-permute-done((bf16[80,512]{1,0:T(8,128)(2,1)S(1)}, bf16[80,512]{1,0:T(8,128)(2,1)S(1)}, u32[]{:S(2)}, u32[]{:S(2)}) %collective-permute-start.2) | collective-permute-done | bytes 81952 | tf_op jit(solution)/shard_map/ppermute | solution.py:22
  26.5 0.0 copy-start
  26.5 0.9 %copy-done = bf16[80,512]{1,0:T(8,128)(2,1)S(1)} copy-done((bf16[80,512]{1,0:T(8,128)(2,1)S(1)}, bf16[80,512]{1,0:T(8,128)(2,1)}, u32[]{:S(2)}) %copy-start) | copy-done | bytes 81944
  27.3 32.8 %factor.1 = (f32[1024,1024]{1,0:T(8,128)}, bf16[32,1024]{1,0:T(8,128)(2,1)}, f32[1,32]{1,0:T(1,128)S(1)}) custom-call(s32[1]{0:T(128)} %bitcast.me_ref, bf16[80,512]{1,0:T(8,128)(2,1)S(1)} %copy-done, bf16[80,512]{1,0:T(8,128)(2,1)S(1)} %collective-permute-done.refs_1_, bf16[80,512]{1,0:T(8,128)(2,1)S(1)} %collective-permute-done.1.refs_2_, ...), custom_call_target="tpu_custom_call" | custom-call | tf_op jit(solution)/shard_map/factor/pallas_call | solution.py:352
  60.1 0.1 collective-permute-start.9
  60.2 1.6 %collective-permute-start.8 = (f32[1,32]{1,0:T(1,128)S(1)}, f32[1,32]{1,0:T(1,128)S(1)}, u32[]{:S(2)}, u32[]{:S(2)}) collective-permute-start(f32[1,32]{1,0:T(1,128)S(1)} %get-tuple-element.8), channel_id=1, source_target_pairs={{0,2},{1,3},{2,0},{3,1},{4,6},{5,7},{6,4},{7,5},{8,10},{9,11},{10,... | collective-permute-start | bytes 392 | tf_op jit(solution)/shard_map/ppermute | solution.py:22
  61.8 0.3 collective-permute-start.7
  62.1 1.1 %collective-permute-done.9 = f32[1,32]{1,0:T(1,128)S(1)} collective-permute-done((f32[1,32]{1,0:T(1,128)S(1)}, f32[1,32]{1,0:T(1,128)S(1)}, u32[]{:S(2)}, u32[]{:S(2)}) %collective-permute-start.9) | collective-permute-done | bytes 160 | tf_op jit(solution)/shard_map/ppermute | solution.py:22
  63.2 0.7 %collective-permute-done.8 = f32[1,32]{1,0:T(1,128)S(1)} collective-permute-done((f32[1,32]{1,0:T(1,128)S(1)}, f32[1,32]{1,0:T(1,128)S(1)}, u32[]{:S(2)}, u32[]{:S(2)}) %collective-permute-start.8) | collective-permute-done | bytes 160 | tf_op jit(solution)/shard_map/ppermute | solution.py:22
  63.8 0.0 collective-permute-done.7
  63.8 0.5 add_bitcast_fusion
Async XLA Ops:
  8.3 8.3 %collective-permute-start.5 = (bf16[80,512]{1,0:T(8,128)(2,1)}, bf16[80,512]{1,0:T(8,128)(2,1)S(1)}, u32[]{:S(2)}, u32[]{:S(2)}) collective-permute-start(bf16[80,512]{1,0:T(8,128)(2,1)} %project.1.refs_0_), channel_id=1, source_target_pairs={{0,24},{4,28},{8,16},{12,20},{16,8},{20,12},{24,0},{28,4},{1,25},{... | collective-permute-start | bytes 245768 | tf_op jit(solution)/shard_map/ppermute | solution.py:22
  13.4 7.1 %collective-permute-start.3 = (bf16[80,512]{1,0:T(8,128)(2,1)}, bf16[80,512]{1,0:T(8,128)(2,1)S(1)}, u32[]{:S(2)}, u32[]{:S(2)}) collective-permute-start(bf16[80,512]{1,0:T(8,128)(2,1)} %project.1.refs_0_), channel_id=1, source_target_pairs={{0,16},{4,20},{8,24},{12,28},{16,0},{20,4},{24,8},{28,12},{1,17},{... | collective-permute-start | bytes 245768 | tf_op jit(solution)/shard_map/ppermute | solution.py:22
  13.4 8.6 %collective-permute-start.1 = (bf16[80,512]{1,0:T(8,128)(2,1)}, bf16[80,512]{1,0:T(8,128)(2,1)S(1)}, u32[]{:S(2)}, u32[]{:S(2)}) collective-permute-start(bf16[80,512]{1,0:T(8,128)(2,1)} %project.1.refs_0_), channel_id=1, source_target_pairs={{0,8},{4,12},{8,0},{12,4},{16,24},{20,28},{24,16},{28,20},{1,9},{5... | collective-permute-start | bytes 245768 | tf_op jit(solution)/shard_map/ppermute | solution.py:22
  14.1 8.5 %collective-permute-start = (bf16[80,512]{1,0:T(8,128)(2,1)}, bf16[80,512]{1,0:T(8,128)(2,1)S(1)}, u32[]{:S(2)}, u32[]{:S(2)}) collective-permute-start(bf16[80,512]{1,0:T(8,128)(2,1)} %project.1.refs_0_), channel_id=1, source_target_pairs={{0,4},{4,0},{8,12},{12,8},{16,20},{20,16},{24,28},{28,24},{1,5},{5... | collective-permute-start | bytes 245768 | tf_op jit(solution)/shard_map/ppermute | solution.py:22
  16.7 5.9 %collective-permute-start.6 = (bf16[80,512]{1,0:T(8,128)(2,1)S(1)}, bf16[80,512]{1,0:T(8,128)(2,1)S(1)}, u32[]{:S(2)}, u32[]{:S(2)}) collective-permute-start(bf16[80,512]{1,0:T(8,128)(2,1)S(1)} %collective-permute-done.5.refs_6_), channel_id=1, source_target_pairs={{0,4},{4,0},{8,12},{12,8},{16,20},{20,16},{24,28},{28,24},{1,5},{5... | collective-permute-start | bytes 245768 | tf_op jit(solution)/shard_map/ppermute | solution.py:22
  20.5 5.0 %collective-permute-start.4 = (bf16[80,512]{1,0:T(8,128)(2,1)S(1)}, bf16[80,512]{1,0:T(8,128)(2,1)S(1)}, u32[]{:S(2)}, u32[]{:S(2)}) collective-permute-start(bf16[80,512]{1,0:T(8,128)(2,1)S(1)} %collective-permute-done.3.refs_4_), channel_id=1, source_target_pairs={{0,4},{4,0},{8,12},{12,8},{16,20},{20,16},{24,28},{28,24},{1,5},{5... | collective-permute-start | bytes 245768 | tf_op jit(solution)/shard_map/ppermute | solution.py:22
  22.0 4.4 %collective-permute-start.2 = (bf16[80,512]{1,0:T(8,128)(2,1)S(1)}, bf16[80,512]{1,0:T(8,128)(2,1)S(1)}, u32[]{:S(2)}, u32[]{:S(2)}) collective-permute-start(bf16[80,512]{1,0:T(8,128)(2,1)S(1)} %collective-permute-done.1.refs_2_), channel_id=1, source_target_pairs={{0,4},{4,0},{8,12},{12,8},{16,20},{20,16},{24,28},{28,24},{1,5},{5... | collective-permute-start | bytes 245768 | tf_op jit(solution)/shard_map/ppermute | solution.py:22
  26.5 0.9 %copy-start = (bf16[80,512]{1,0:T(8,128)(2,1)S(1)}, bf16[80,512]{1,0:T(8,128)(2,1)}, u32[]{:S(2)}) copy-start(bf16[80,512]{1,0:T(8,128)(2,1)} %project.1.refs_0_) | copy-start | bytes 245764
  60.1 3.0 %collective-permute-start.9 = (f32[1,32]{1,0:T(1,128)S(1)}, f32[1,32]{1,0:T(1,128)S(1)}, u32[]{:S(2)}, u32[]{:S(2)}) collective-permute-start(f32[1,32]{1,0:T(1,128)S(1)} %get-tuple-element.8), channel_id=1, source_target_pairs={{0,3},{1,2},{2,1},{3,0},{4,7},{5,6},{6,5},{7,4},{8,11},{9,10},{10,... | collective-permute-start | bytes 392 | tf_op jit(solution)/shard_map/ppermute | solution.py:22
  60.2 3.6 %collective-permute-start.8 = (f32[1,32]{1,0:T(1,128)S(1)}, f32[1,32]{1,0:T(1,128)S(1)}, u32[]{:S(2)}, u32[]{:S(2)}) collective-permute-start(f32[1,32]{1,0:T(1,128)S(1)} %get-tuple-element.8), channel_id=1, source_target_pairs={{0,2},{1,3},{2,0},{3,1},{4,6},{5,7},{6,4},{7,5},{8,10},{9,11},{10,... | collective-permute-start | bytes 392 | tf_op jit(solution)/shard_map/ppermute | solution.py:22
  61.8 2.0 %collective-permute-start.7 = (f32[1,32]{1,0:T(1,128)S(1)}, f32[1,32]{1,0:T(1,128)S(1)}, u32[]{:S(2)}, u32[]{:S(2)}) collective-permute-start(f32[1,32]{1,0:T(1,128)S(1)} %get-tuple-element.8), channel_id=1, source_target_pairs={{0,1},{1,0},{2,3},{3,2},{4,5},{5,4},{6,7},{7,6},{8,9},{9,8},{10,11... | collective-permute-start | bytes 392 | tf_op jit(solution)/shard_map/ppermute | solution.py:22

commit v4 on v3

--- a/solution.py
+++ b/solution.py
@@ -227,7 +227,7 @@
     n_rep = len(pieces)
     docs = p_ref.shape[0]
     rows = docs // n_rep
-    tokens = p_ref.shape[1] // 4
+    tokens = p_ref.shape[1] // 2
     me = me_ref[0]
     for d in range(n_rep):
         tok_ref[me ^ d] = pieces[d][...]
@@ -246,8 +246,6 @@
             last = target[:, tokens - 1 : tokens]
             member = jnp.where(doc == target, 1.0, 0.0).astype(jnp.bfloat16)
             p_ref[:, h * tokens : (h + 1) * tokens] = member
-            p_ref[:, (h + 2) * tokens : (h + 3) * tokens] = member
-        len_ref[...] += dot_n(ones, p_ref[:, 0 : 2 * tokens])
         lefts = [tok_ref[2 * pair + h, 0:side, :].astype(jnp.float32) for h in range(2)]
         rights = [tok_ref[2 * pair + h, side : 2 * side, :].astype(jnp.float32) for h in range(2)]
         for q in range(0, side, 8):
@@ -259,8 +257,13 @@
                 )
                 highs.append(outer.astype(jnp.bfloat16))
                 lows.append((outer - highs[h].astype(jnp.float32)).astype(jnp.bfloat16))
-            parts = jnp.concatenate(highs + lows, 1)
-            sum_ref[q * side : q * side + tall, :] += dot_n(parts, p_ref[...])
+            parts = [jnp.concatenate(highs, 1), jnp.concatenate(lows, 1)]
+            if q == 0:
+                parts.append(ones)
+            both = dot_n(jnp.concatenate(parts, 0), p_ref[...])
+            if q == 0:
+                len_ref[...] += both[2 * tall :]
+            sum_ref[q * side : q * side + tall, :] += both[0:tall] + both[tall : 2 * tall]
         return last
 
     lax.fori_loop(0, n_rep // 2, add_tokens, jnp.zeros((1, 1), jnp.float32))
@@ -362,7 +365,7 @@
             pltpu.VMEM((n_rep, height, tokens), jnp.bfloat16),
             pltpu.VMEM((width, docs), jnp.float32),
             pltpu.VMEM((16, docs), jnp.float32),
-            pltpu.VMEM((docs, 4 * tokens), jnp.bfloat16),
+            pltpu.VMEM((docs, 2 * tokens), jnp.bfloat16),
             pltpu.VMEM((width, docs), jnp.bfloat16),
             pltpu.VMEM((width, width), jnp.float32),
             pltpu.VMEM((3, width, width), jnp.bfloat16),

time: 64.5 us -> 63.9 us (level)
  Pallas kernels: 40.5 us -> 39.8 us
    pallas_call x1, Pallas kernels: 32.8 us -> 32.1 us  [factor_and_solve(): pl.pallas_call(functools.partial(factor_kernel, width), out_shape=[jax.Sh...]
where the time goes in v4:
time: 63.9 us; the launch traced here: 63.7 us
  Pallas kernels  39.8 us (62%)
  starting transfers between devices  13.1 us (21%)
  waiting for transfers between devices  8.7 us (14%)
  local copies, waits for them, and re-layouts  0.89 us (1%)
  between operations  0.67 us (1%)
    pallas_call x1, Pallas kernels, factor_and_solve(): pl.pallas_call(functools.partial(factor_kernel, width), out_shape=[jax.Sh...  32.1 us
    ppermute x10, starting transfers between devices, swapped(): return lax.ppermute(block, axis, [(i, i ^ distance) for i in devices])  13.1 us
    ppermute x10, waiting for transfers between devices, swapped(): return lax.ppermute(block, axis, [(i, i ^ distance) for i in devices])  8.7 us
    pallas_call x1, Pallas kernels, project(): pl.pallas_call(project_kernel, out_shape=jax.ShapeDtypeStruct((2 * width...  7.7 us
  transfers between devices with their start and end apart: 10, of which 6 were waited for; matrix products, arithmetic and copies ran while one was open for 0% of the time, Pallas kernels for 0%

profile of v4, /device:TPU:0, one launch (start us, length us, event | category | flops | bytes accessed | tf_op | source)
XLA Modules:
  0.0 63.7 jit_solution(9878658912907681233)
XLA Ops:
  0.6 7.7 %project.1.refs_0_ = bf16[80,512]{1,0:T(8,128)(2,1)} custom-call(bf16[512,8192]{1,0:T(8,128)(2,1)} %bitcast.11, bf16[512,8192]{1,0:T(8,128)(2,1)} %bitcast.12, bf16[32,8192]{1,0:T(8,128)(2,1)} %bitcast.13, bf16[32,8192]{1,0:T(8,128)(2,1)} %bitcast.14, s32[1,512]{1,0:T(1,128)} %bitcast.15, s32[1,62]{1,0:T(1,128)} %bitcast.16), custom_call_target="tpu_custom_call" | custom-call | tf_op jit(solution)/shard_map/project/pallas_call | solution.py:118
  8.3 5.1 %collective-permute-start.5 = (bf16[80,512]{1,0:T(8,128)(2,1)}, bf16[80,512]{1,0:T(8,128)(2,1)S(1)}, u32[]{:S(2)}, u32[]{:S(2)}) collective-permute-start(bf16[80,512]{1,0:T(8,128)(2,1)} %project.1.refs_0_), channel_id=1, source_target_pairs={{0,24},{4,28},{8,16},{12,20},{16,8},{20,12},{24,0},{28,4},{1,25},{... | collective-permute-start | bytes 245768 | tf_op jit(solution)/shard_map/ppermute | solution.py:22
  13.4 0.0 collective-permute-start.3
  13.4 0.6 %collective-permute-start.1 = (bf16[80,512]{1,0:T(8,128)(2,1)}, bf16[80,512]{1,0:T(8,128)(2,1)S(1)}, u32[]{:S(2)}, u32[]{:S(2)}) collective-permute-start(bf16[80,512]{1,0:T(8,128)(2,1)} %project.1.refs_0_), channel_id=1, source_target_pairs={{0,8},{4,12},{8,0},{12,4},{16,24},{20,28},{24,16},{28,20},{1,9},{5... | collective-permute-start | bytes 245768 | tf_op jit(solution)/shard_map/ppermute | solution.py:22
  14.1 1.6 %collective-permute-start = (bf16[80,512]{1,0:T(8,128)(2,1)}, bf16[80,512]{1,0:T(8,128)(2,1)S(1)}, u32[]{:S(2)}, u32[]{:S(2)}) collective-permute-start(bf16[80,512]{1,0:T(8,128)(2,1)} %project.1.refs_0_), channel_id=1, source_target_pairs={{0,4},{4,0},{8,12},{12,8},{16,20},{20,16},{24,28},{28,24},{1,5},{5... | collective-permute-start | bytes 245768 | tf_op jit(solution)/shard_map/ppermute | solution.py:22
  15.7 1.0 %collective-permute-done.5.refs_6_ = bf16[80,512]{1,0:T(8,128)(2,1)S(1)} collective-permute-done((bf16[80,512]{1,0:T(8,128)(2,1)}, bf16[80,512]{1,0:T(8,128)(2,1)S(1)}, u32[]{:S(2)}, u32[]{:S(2)}) %collective-permute-start.5) | collective-permute-done | bytes 81952 | tf_op jit(solution)/shard_map/ppermute | solution.py:22
  16.7 1.8 %collective-permute-start.6 = (bf16[80,512]{1,0:T(8,128)(2,1)S(1)}, bf16[80,512]{1,0:T(8,128)(2,1)S(1)}, u32[]{:S(2)}, u32[]{:S(2)}) collective-permute-start(bf16[80,512]{1,0:T(8,128)(2,1)S(1)} %collective-permute-done.5.refs_6_), channel_id=1, source_target_pairs={{0,4},{4,0},{8,12},{12,8},{16,20},{20,16},{24,28},{28,24},{1,5},{5... | collective-permute-start | bytes 245768 | tf_op jit(solution)/shard_map/ppermute | solution.py:22
  18.4 2.1 %collective-permute-done.3.refs_4_ = bf16[80,512]{1,0:T(8,128)(2,1)S(1)} collective-permute-done((bf16[80,512]{1,0:T(8,128)(2,1)}, bf16[80,512]{1,0:T(8,128)(2,1)S(1)}, u32[]{:S(2)}, u32[]{:S(2)}) %collective-permute-start.3) | collective-permute-done | bytes 81952 | tf_op jit(solution)/shard_map/ppermute | solution.py:22
  20.5 1.5 %collective-permute-start.4 = (bf16[80,512]{1,0:T(8,128)(2,1)S(1)}, bf16[80,512]{1,0:T(8,128)(2,1)S(1)}, u32[]{:S(2)}, u32[]{:S(2)}) collective-permute-start(bf16[80,512]{1,0:T(8,128)(2,1)S(1)} %collective-permute-done.3.refs_4_), channel_id=1, source_target_pairs={{0,4},{4,0},{8,12},{12,8},{16,20},{20,16},{24,28},{28,24},{1,5},{5... | collective-permute-start | bytes 245768 | tf_op jit(solution)/shard_map/ppermute | solution.py:22
  22.0 0.0 collective-permute-done.1.refs_2_
  22.0 0.5 collective-permute-start.2
  22.5 0.0 collective-permute-done.refs_1_
  22.6 0.0 collective-permute-done.6.refs_7_
  22.6 3.0 %collective-permute-done.4.refs_5_ = bf16[80,512]{1,0:T(8,128)(2,1)S(1)} collective-permute-done((bf16[80,512]{1,0:T(8,128)(2,1)S(1)}, bf16[80,512]{1,0:T(8,128)(2,1)S(1)}, u32[]{:S(2)}, u32[]{:S(2)}) %collective-permute-start.4) | collective-permute-done | bytes 81952 | tf_op jit(solution)/shard_map/ppermute | solution.py:22
  25.5 0.9 %collective-permute-done.2.refs_3_ = bf16[80,512]{1,0:T(8,128)(2,1)S(1)} collective-permute-done((bf16[80,512]{1,0:T(8,128)(2,1)S(1)}, bf16[80,512]{1,0:T(8,128)(2,1)S(1)}, u32[]{:S(2)}, u32[]{:S(2)}) %collective-permute-start.2) | collective-permute-done | bytes 81952 | tf_op jit(solution)/shard_map/ppermute | solution.py:22
  26.5 0.0 copy-start
  26.5 0.9 %copy-done = bf16[80,512]{1,0:T(8,128)(2,1)S(1)} copy-done((bf16[80,512]{1,0:T(8,128)(2,1)S(1)}, bf16[80,512]{1,0:T(8,128)(2,1)}, u32[]{:S(2)}) %copy-start) | copy-done | bytes 81944
  27.3 32.1 %factor.1 = (f32[1024,1024]{1,0:T(8,128)}, bf16[32,1024]{1,0:T(8,128)(2,1)}, f32[1,32]{1,0:T(1,128)S(1)}) custom-call(s32[1]{0:T(128)} %bitcast.me_ref, bf16[80,512]{1,0:T(8,128)(2,1)S(1)} %copy-done, bf16[80,512]{1,0:T(8,128)(2,1)S(1)} %collective-permute-done.refs_1_, bf16[80,512]{1,0:T(8,128)(2,1)S(1)} %collective-permute-done.1.refs_2_, ...), custom_call_target="tpu_custom_call" | custom-call | tf_op jit(solution)/shard_map/factor/pallas_call | solution.py:355
  59.5 0.1 collective-permute-start.9
  59.6 1.6 %collective-permute-start.8 = (f32[1,32]{1,0:T(1,128)S(1)}, f32[1,32]{1,0:T(1,128)S(1)}, u32[]{:S(2)}, u32[]{:S(2)}) collective-permute-start(f32[1,32]{1,0:T(1,128)S(1)} %get-tuple-element.8), channel_id=1, source_target_pairs={{0,2},{1,3},{2,0},{3,1},{4,6},{5,7},{6,4},{7,5},{8,10},{9,11},{10,... | collective-permute-start | bytes 392 | tf_op jit(solution)/shard_map/ppermute | solution.py:22
  61.1 0.3 collective-permute-start.7
  61.4 1.1 %collective-permute-done.9 = f32[1,32]{1,0:T(1,128)S(1)} collective-permute-done((f32[1,32]{1,0:T(1,128)S(1)}, f32[1,32]{1,0:T(1,128)S(1)}, u32[]{:S(2)}, u32[]{:S(2)}) %collective-permute-start.9) | collective-permute-done | bytes 160 | tf_op jit(solution)/shard_map/ppermute | solution.py:22
  62.5 0.7 %collective-permute-done.8 = f32[1,32]{1,0:T(1,128)S(1)} collective-permute-done((f32[1,32]{1,0:T(1,128)S(1)}, f32[1,32]{1,0:T(1,128)S(1)}, u32[]{:S(2)}, u32[]{:S(2)}) %collective-permute-start.8) | collective-permute-done | bytes 160 | tf_op jit(solution)/shard_map/ppermute | solution.py:22
  63.2 0.0 collective-permute-done.7
  63.2 0.5 add_bitcast_fusion
Async XLA Ops:
  8.3 8.3 %collective-permute-start.5 = (bf16[80,512]{1,0:T(8,128)(2,1)}, bf16[80,512]{1,0:T(8,128)(2,1)S(1)}, u32[]{:S(2)}, u32[]{:S(2)}) collective-permute-start(bf16[80,512]{1,0:T(8,128)(2,1)} %project.1.refs_0_), channel_id=1, source_target_pairs={{0,24},{4,28},{8,16},{12,20},{16,8},{20,12},{24,0},{28,4},{1,25},{... | collective-permute-start | bytes 245768 | tf_op jit(solution)/shard_map/ppermute | solution.py:22
  13.4 7.1 %collective-permute-start.3 = (bf16[80,512]{1,0:T(8,128)(2,1)}, bf16[80,512]{1,0:T(8,128)(2,1)S(1)}, u32[]{:S(2)}, u32[]{:S(2)}) collective-permute-start(bf16[80,512]{1,0:T(8,128)(2,1)} %project.1.refs_0_), channel_id=1, source_target_pairs={{0,16},{4,20},{8,24},{12,28},{16,0},{20,4},{24,8},{28,12},{1,17},{... | collective-permute-start | bytes 245768 | tf_op jit(solution)/shard_map/ppermute | solution.py:22
  13.4 8.6 %collective-permute-start.1 = (bf16[80,512]{1,0:T(8,128)(2,1)}, bf16[80,512]{1,0:T(8,128)(2,1)S(1)}, u32[]{:S(2)}, u32[]{:S(2)}) collective-permute-start(bf16[80,512]{1,0:T(8,128)(2,1)} %project.1.refs_0_), channel_id=1, source_target_pairs={{0,8},{4,12},{8,0},{12,4},{16,24},{20,28},{24,16},{28,20},{1,9},{5... | collective-permute-start | bytes 245768 | tf_op jit(solution)/shard_map/ppermute | solution.py:22
  14.1 8.5 %collective-permute-start = (bf16[80,512]{1,0:T(8,128)(2,1)}, bf16[80,512]{1,0:T(8,128)(2,1)S(1)}, u32[]{:S(2)}, u32[]{:S(2)}) collective-permute-start(bf16[80,512]{1,0:T(8,128)(2,1)} %project.1.refs_0_), channel_id=1, source_target_pairs={{0,4},{4,0},{8,12},{12,8},{16,20},{20,16},{24,28},{28,24},{1,5},{5... | collective-permute-start | bytes 245768 | tf_op jit(solution)/shard_map/ppermute | solution.py:22
  16.7 5.9 %collective-permute-start.6 = (bf16[80,512]{1,0:T(8,128)(2,1)S(1)}, bf16[80,512]{1,0:T(8,128)(2,1)S(1)}, u32[]{:S(2)}, u32[]{:S(2)}) collective-permute-start(bf16[80,512]{1,0:T(8,128)(2,1)S(1)} %collective-permute-done.5.refs_6_), channel_id=1, source_target_pairs={{0,4},{4,0},{8,12},{12,8},{16,20},{20,16},{24,28},{28,24},{1,5},{5... | collective-permute-start | bytes 245768 | tf_op jit(solution)/shard_map/ppermute | solution.py:22
  20.5 5.0 %collective-permute-start.4 = (bf16[80,512]{1,0:T(8,128)(2,1)S(1)}, bf16[80,512]{1,0:T(8,128)(2,1)S(1)}, u32[]{:S(2)}, u32[]{:S(2)}) collective-permute-start(bf16[80,512]{1,0:T(8,128)(2,1)S(1)} %collective-permute-done.3.refs_4_), channel_id=1, source_target_pairs={{0,4},{4,0},{8,12},{12,8},{16,20},{20,16},{24,28},{28,24},{1,5},{5... | collective-permute-start | bytes 245768 | tf_op jit(solution)/shard_map/ppermute | solution.py:22
  22.0 4.4 %collective-permute-start.2 = (bf16[80,512]{1,0:T(8,128)(2,1)S(1)}, bf16[80,512]{1,0:T(8,128)(2,1)S(1)}, u32[]{:S(2)}, u32[]{:S(2)}) collective-permute-start(bf16[80,512]{1,0:T(8,128)(2,1)S(1)} %collective-permute-done.1.refs_2_), channel_id=1, source_target_pairs={{0,4},{4,0},{8,12},{12,8},{16,20},{20,16},{24,28},{28,24},{1,5},{5... | collective-permute-start | bytes 245768 | tf_op jit(solution)/shard_map/ppermute | solution.py:22
  26.5 0.9 %copy-start = (bf16[80,512]{1,0:T(8,128)(2,1)S(1)}, bf16[80,512]{1,0:T(8,128)(2,1)}, u32[]{:S(2)}) copy-start(bf16[80,512]{1,0:T(8,128)(2,1)} %project.1.refs_0_) | copy-start | bytes 245764
  59.5 3.0 %collective-permute-start.9 = (f32[1,32]{1,0:T(1,128)S(1)}, f32[1,32]{1,0:T(1,128)S(1)}, u32[]{:S(2)}, u32[]{:S(2)}) collective-permute-start(f32[1,32]{1,0:T(1,128)S(1)} %get-tuple-element.8), channel_id=1, source_target_pairs={{0,3},{1,2},{2,1},{3,0},{4,7},{5,6},{6,5},{7,4},{8,11},{9,10},{10,... | collective-permute-start | bytes 392 | tf_op jit(solution)/shard_map/ppermute | solution.py:22
  59.6 3.6 %collective-permute-start.8 = (f32[1,32]{1,0:T(1,128)S(1)}, f32[1,32]{1,0:T(1,128)S(1)}, u32[]{:S(2)}, u32[]{:S(2)}) collective-permute-start(f32[1,32]{1,0:T(1,128)S(1)} %get-tuple-element.8), channel_id=1, source_target_pairs={{0,2},{1,3},{2,0},{3,1},{4,6},{5,7},{6,4},{7,5},{8,10},{9,11},{10,... | collective-permute-start | bytes 392 | tf_op jit(solution)/shard_map/ppermute | solution.py:22
  61.1 2.0 %collective-permute-start.7 = (f32[1,32]{1,0:T(1,128)S(1)}, f32[1,32]{1,0:T(1,128)S(1)}, u32[]{:S(2)}, u32[]{:S(2)}) collective-permute-start(f32[1,32]{1,0:T(1,128)S(1)} %get-tuple-element.8), channel_id=1, source_target_pairs={{0,1},{1,0},{2,3},{3,2},{4,5},{5,4},{6,7},{7,6},{8,9},{9,8},{10,11... | collective-permute-start | bytes 392 | tf_op jit(solution)/shard_map/ppermute | solution.py:22

commit v5 on v4

--- a/solution.py
+++ b/solution.py
@@ -212,7 +212,7 @@
             right = jnp.where(
                 (tall_lane > row) & (tall_lane < b), 0.0, jnp.where(tall_lane == row, scale, block)
             )
-            update = dot_t(block, right)
+            update = dot_parts(split(block), split(right), 0)
             for i in range(h + n, groups):
                 x[i] = jnp.where((lane >= a) & (lane < b), 0.0, x[i]) - update[8 * i : 8 * i + 8, :]
         for q in range(n):

time: 63.9 us -> 63.2 us (0.989)
  Pallas kernels: 39.8 us -> 39.1 us
    pallas_call x1, Pallas kernels: 32.1 us -> 31.4 us  [factor_and_solve(): pl.pallas_call(functools.partial(factor_kernel, width), out_shape=[jax.Sh...]
where the time goes in v5:
time: 63.2 us; the launch traced here: 63 us
  Pallas kernels  39.1 us (62%)
  starting transfers between devices  13.1 us (21%)
  waiting for transfers between devices  8.7 us (14%)
  local copies, waits for them, and re-layouts  0.89 us (1%)
  between operations  0.67 us (1%)
    pallas_call x1, Pallas kernels, factor_and_solve(): pl.pallas_call(functools.partial(factor_kernel, width), out_shape=[jax.Sh...  31.4 us
    ppermute x10, starting transfers between devices, swapped(): return lax.ppermute(block, axis, [(i, i ^ distance) for i in devices])  13.1 us
    ppermute x10, waiting for transfers between devices, swapped(): return lax.ppermute(block, axis, [(i, i ^ distance) for i in devices])  8.7 us
    pallas_call x1, Pallas kernels, project(): pl.pallas_call(project_kernel, out_shape=jax.ShapeDtypeStruct((2 * width...  7.7 us
  transfers between devices with their start and end apart: 10, of which 6 were waited for; matrix products, arithmetic and copies ran while one was open for 0% of the time, Pallas kernels for 0%

profile of v5, /device:TPU:0, one launch (start us, length us, event | category | flops | bytes accessed | tf_op | source)
XLA Modules:
  0.0 63.0 jit_solution(12954117833248230501)
XLA Ops:
  0.6 7.7 %project.1.refs_0_ = bf16[80,512]{1,0:T(8,128)(2,1)} custom-call(bf16[512,8192]{1,0:T(8,128)(2,1)} %bitcast.11, bf16[512,8192]{1,0:T(8,128)(2,1)} %bitcast.12, bf16[32,8192]{1,0:T(8,128)(2,1)} %bitcast.13, bf16[32,8192]{1,0:T(8,128)(2,1)} %bitcast.14, s32[1,512]{1,0:T(1,128)} %bitcast.15, s32[1,62]{1,0:T(1,128)} %bitcast.16), custom_call_target="tpu_custom_call" | custom-call | tf_op jit(solution)/shard_map/project/pallas_call | solution.py:118
  8.3 5.1 %collective-permute-start.5 = (bf16[80,512]{1,0:T(8,128)(2,1)}, bf16[80,512]{1,0:T(8,128)(2,1)S(1)}, u32[]{:S(2)}, u32[]{:S(2)}) collective-permute-start(bf16[80,512]{1,0:T(8,128)(2,1)} %project.1.refs_0_), channel_id=1, source_target_pairs={{0,24},{4,28},{8,16},{12,20},{16,8},{20,12},{24,0},{28,4},{1,25},{... | collective-permute-start | bytes 245768 | tf_op jit(solution)/shard_map/ppermute | solution.py:22
  13.4 0.0 collective-permute-start.3
  13.4 0.6 %collective-permute-start.1 = (bf16[80,512]{1,0:T(8,128)(2,1)}, bf16[80,512]{1,0:T(8,128)(2,1)S(1)}, u32[]{:S(2)}, u32[]{:S(2)}) collective-permute-start(bf16[80,512]{1,0:T(8,128)(2,1)} %project.1.refs_0_), channel_id=1, source_target_pairs={{0,8},{4,12},{8,0},{12,4},{16,24},{20,28},{24,16},{28,20},{1,9},{5... | collective-permute-start | bytes 245768 | tf_op jit(solution)/shard_map/ppermute | solution.py:22
  14.1 1.6 %collective-permute-start = (bf16[80,512]{1,0:T(8,128)(2,1)}, bf16[80,512]{1,0:T(8,128)(2,1)S(1)}, u32[]{:S(2)}, u32[]{:S(2)}) collective-permute-start(bf16[80,512]{1,0:T(8,128)(2,1)} %project.1.refs_0_), channel_id=1, source_target_pairs={{0,4},{4,0},{8,12},{12,8},{16,20},{20,16},{24,28},{28,24},{1,5},{5... | collective-permute-start | bytes 245768 | tf_op jit(solution)/shard_map/ppermute | solution.py:22
  15.7 1.0 %collective-permute-done.5.refs_6_ = bf16[80,512]{1,0:T(8,128)(2,1)S(1)} collective-permute-done((bf16[80,512]{1,0:T(8,128)(2,1)}, bf16[80,512]{1,0:T(8,128)(2,1)S(1)}, u32[]{:S(2)}, u32[]{:S(2)}) %collective-permute-start.5) | collective-permute-done | bytes 81952 | tf_op jit(solution)/shard_map/ppermute | solution.py:22
  16.7 1.8 %collective-permute-start.6 = (bf16[80,512]{1,0:T(8,128)(2,1)S(1)}, bf16[80,512]{1,0:T(8,128)(2,1)S(1)}, u32[]{:S(2)}, u32[]{:S(2)}) collective-permute-start(bf16[80,512]{1,0:T(8,128)(2,1)S(1)} %collective-permute-done.5.refs_6_), channel_id=1, source_target_pairs={{0,4},{4,0},{8,12},{12,8},{16,20},{20,16},{24,28},{28,24},{1,5},{5... | collective-permute-start | bytes 245768 | tf_op jit(solution)/shard_map/ppermute | solution.py:22
  18.4 2.1 %collective-permute-done.3.refs_4_ = bf16[80,512]{1,0:T(8,128)(2,1)S(1)} collective-permute-done((bf16[80,512]{1,0:T(8,128)(2,1)}, bf16[80,512]{1,0:T(8,128)(2,1)S(1)}, u32[]{:S(2)}, u32[]{:S(2)}) %collective-permute-start.3) | collective-permute-done | bytes 81952 | tf_op jit(solution)/shard_map/ppermute | solution.py:22
  20.5 1.5 %collective-permute-start.4 = (bf16[80,512]{1,0:T(8,128)(2,1)S(1)}, bf16[80,512]{1,0:T(8,128)(2,1)S(1)}, u32[]{:S(2)}, u32[]{:S(2)}) collective-permute-start(bf16[80,512]{1,0:T(8,128)(2,1)S(1)} %collective-permute-done.3.refs_4_), channel_id=1, source_target_pairs={{0,4},{4,0},{8,12},{12,8},{16,20},{20,16},{24,28},{28,24},{1,5},{5... | collective-permute-start | bytes 245768 | tf_op jit(solution)/shard_map/ppermute | solution.py:22
  22.0 0.0 collective-permute-done.1.refs_2_
  22.0 0.5 collective-permute-start.2
  22.5 0.0 collective-permute-done.refs_1_
  22.6 0.0 collective-permute-done.6.refs_7_
  22.6 3.0 %collective-permute-done.4.refs_5_ = bf16[80,512]{1,0:T(8,128)(2,1)S(1)} collective-permute-done((bf16[80,512]{1,0:T(8,128)(2,1)S(1)}, bf16[80,512]{1,0:T(8,128)(2,1)S(1)}, u32[]{:S(2)}, u32[]{:S(2)}) %collective-permute-start.4) | collective-permute-done | bytes 81952 | tf_op jit(solution)/shard_map/ppermute | solution.py:22
  25.5 0.9 %collective-permute-done.2.refs_3_ = bf16[80,512]{1,0:T(8,128)(2,1)S(1)} collective-permute-done((bf16[80,512]{1,0:T(8,128)(2,1)S(1)}, bf16[80,512]{1,0:T(8,128)(2,1)S(1)}, u32[]{:S(2)}, u32[]{:S(2)}) %collective-permute-start.2) | collective-permute-done | bytes 81952 | tf_op jit(solution)/shard_map/ppermute | solution.py:22
  26.5 0.0 copy-start
  26.5 0.9 %copy-done = bf16[80,512]{1,0:T(8,128)(2,1)S(1)} copy-done((bf16[80,512]{1,0:T(8,128)(2,1)S(1)}, bf16[80,512]{1,0:T(8,128)(2,1)}, u32[]{:S(2)}) %copy-start) | copy-done | bytes 81944
  27.3 31.4 %factor.1 = (f32[1024,1024]{1,0:T(8,128)}, bf16[32,1024]{1,0:T(8,128)(2,1)}, f32[1,32]{1,0:T(1,128)S(1)}) custom-call(s32[1]{0:T(128)} %bitcast.me_ref, bf16[80,512]{1,0:T(8,128)(2,1)S(1)} %copy-done, bf16[80,512]{1,0:T(8,128)(2,1)S(1)} %collective-permute-done.refs_1_, bf16[80,512]{1,0:T(8,128)(2,1)S(1)} %collective-permute-done.1.refs_2_, ...), custom_call_target="tpu_custom_call" | custom-call | tf_op jit(solution)/shard_map/factor/pallas_call | solution.py:355
  58.8 0.1 collective-permute-start.9
  58.9 1.6 %collective-permute-start.8 = (f32[1,32]{1,0:T(1,128)S(1)}, f32[1,32]{1,0:T(1,128)S(1)}, u32[]{:S(2)}, u32[]{:S(2)}) collective-permute-start(f32[1,32]{1,0:T(1,128)S(1)} %get-tuple-element.8), channel_id=1, source_target_pairs={{0,2},{1,3},{2,0},{3,1},{4,6},{5,7},{6,4},{7,5},{8,10},{9,11},{10,... | collective-permute-start | bytes 392 | tf_op jit(solution)/shard_map/ppermute | solution.py:22
  60.5 0.3 collective-permute-start.7
  60.7 1.1 %collective-permute-done.9 = f32[1,32]{1,0:T(1,128)S(1)} collective-permute-done((f32[1,32]{1,0:T(1,128)S(1)}, f32[1,32]{1,0:T(1,128)S(1)}, u32[]{:S(2)}, u32[]{:S(2)}) %collective-permute-start.9) | collective-permute-done | bytes 160 | tf_op jit(solution)/shard_map/ppermute | solution.py:22
  61.8 0.7 %collective-permute-done.8 = f32[1,32]{1,0:T(1,128)S(1)} collective-permute-done((f32[1,32]{1,0:T(1,128)S(1)}, f32[1,32]{1,0:T(1,128)S(1)}, u32[]{:S(2)}, u32[]{:S(2)}) %collective-permute-start.8) | collective-permute-done | bytes 160 | tf_op jit(solution)/shard_map/ppermute | solution.py:22
  62.5 0.0 collective-permute-done.7
  62.5 0.5 add_bitcast_fusion
Async XLA Ops:
  8.3 8.3 %collective-permute-start.5 = (bf16[80,512]{1,0:T(8,128)(2,1)}, bf16[80,512]{1,0:T(8,128)(2,1)S(1)}, u32[]{:S(2)}, u32[]{:S(2)}) collective-permute-start(bf16[80,512]{1,0:T(8,128)(2,1)} %project.1.refs_0_), channel_id=1, source_target_pairs={{0,24},{4,28},{8,16},{12,20},{16,8},{20,12},{24,0},{28,4},{1,25},{... | collective-permute-start | bytes 245768 | tf_op jit(solution)/shard_map/ppermute | solution.py:22
  13.4 7.1 %collective-permute-start.3 = (bf16[80,512]{1,0:T(8,128)(2,1)}, bf16[80,512]{1,0:T(8,128)(2,1)S(1)}, u32[]{:S(2)}, u32[]{:S(2)}) collective-permute-start(bf16[80,512]{1,0:T(8,128)(2,1)} %project.1.refs_0_), channel_id=1, source_target_pairs={{0,16},{4,20},{8,24},{12,28},{16,0},{20,4},{24,8},{28,12},{1,17},{... | collective-permute-start | bytes 245768 | tf_op jit(solution)/shard_map/ppermute | solution.py:22
  13.4 8.6 %collective-permute-start.1 = (bf16[80,512]{1,0:T(8,128)(2,1)}, bf16[80,512]{1,0:T(8,128)(2,1)S(1)}, u32[]{:S(2)}, u32[]{:S(2)}) collective-permute-start(bf16[80,512]{1,0:T(8,128)(2,1)} %project.1.refs_0_), channel_id=1, source_target_pairs={{0,8},{4,12},{8,0},{12,4},{16,24},{20,28},{24,16},{28,20},{1,9},{5... | collective-permute-start | bytes 245768 | tf_op jit(solution)/shard_map/ppermute | solution.py:22
  14.1 8.5 %collective-permute-start = (bf16[80,512]{1,0:T(8,128)(2,1)}, bf16[80,512]{1,0:T(8,128)(2,1)S(1)}, u32[]{:S(2)}, u32[]{:S(2)}) collective-permute-start(bf16[80,512]{1,0:T(8,128)(2,1)} %project.1.refs_0_), channel_id=1, source_target_pairs={{0,4},{4,0},{8,12},{12,8},{16,20},{20,16},{24,28},{28,24},{1,5},{5... | collective-permute-start | bytes 245768 | tf_op jit(solution)/shard_map/ppermute | solution.py:22
  16.7 5.9 %collective-permute-start.6 = (bf16[80,512]{1,0:T(8,128)(2,1)S(1)}, bf16[80,512]{1,0:T(8,128)(2,1)S(1)}, u32[]{:S(2)}, u32[]{:S(2)}) collective-permute-start(bf16[80,512]{1,0:T(8,128)(2,1)S(1)} %collective-permute-done.5.refs_6_), channel_id=1, source_target_pairs={{0,4},{4,0},{8,12},{12,8},{16,20},{20,16},{24,28},{28,24},{1,5},{5... | collective-permute-start | bytes 245768 | tf_op jit(solution)/shard_map/ppermute | solution.py:22
  20.5 5.0 %collective-permute-start.4 = (bf16[80,512]{1,0:T(8,128)(2,1)S(1)}, bf16[80,512]{1,0:T(8,128)(2,1)S(1)}, u32[]{:S(2)}, u32[]{:S(2)}) collective-permute-start(bf16[80,512]{1,0:T(8,128)(2,1)S(1)} %collective-permute-done.3.refs_4_), channel_id=1, source_target_pairs={{0,4},{4,0},{8,12},{12,8},{16,20},{20,16},{24,28},{28,24},{1,5},{5... | collective-permute-start | bytes 245768 | tf_op jit(solution)/shard_map/ppermute | solution.py:22
  22.0 4.4 %collective-permute-start.2 = (bf16[80,512]{1,0:T(8,128)(2,1)S(1)}, bf16[80,512]{1,0:T(8,128)(2,1)S(1)}, u32[]{:S(2)}, u32[]{:S(2)}) collective-permute-start(bf16[80,512]{1,0:T(8,128)(2,1)S(1)} %collective-permute-done.1.refs_2_), channel_id=1, source_target_pairs={{0,4},{4,0},{8,12},{12,8},{16,20},{20,16},{24,28},{28,24},{1,5},{5... | collective-permute-start | bytes 245768 | tf_op jit(solution)/shard_map/ppermute | solution.py:22
  26.5 0.9 %copy-start = (bf16[80,512]{1,0:T(8,128)(2,1)S(1)}, bf16[80,512]{1,0:T(8,128)(2,1)}, u32[]{:S(2)}) copy-start(bf16[80,512]{1,0:T(8,128)(2,1)} %project.1.refs_0_) | copy-start | bytes 245764
  58.8 3.0 %collective-permute-start.9 = (f32[1,32]{1,0:T(1,128)S(1)}, f32[1,32]{1,0:T(1,128)S(1)}, u32[]{:S(2)}, u32[]{:S(2)}) collective-permute-start(f32[1,32]{1,0:T(1,128)S(1)} %get-tuple-element.8), channel_id=1, source_target_pairs={{0,3},{1,2},{2,1},{3,0},{4,7},{5,6},{6,5},{7,4},{8,11},{9,10},{10,... | collective-permute-start | bytes 392 | tf_op jit(solution)/shard_map/ppermute | solution.py:22
  58.9 3.6 %collective-permute-start.8 = (f32[1,32]{1,0:T(1,128)S(1)}, f32[1,32]{1,0:T(1,128)S(1)}, u32[]{:S(2)}, u32[]{:S(2)}) collective-permute-start(f32[1,32]{1,0:T(1,128)S(1)} %get-tuple-element.8), channel_id=1, source_target_pairs={{0,2},{1,3},{2,0},{3,1},{4,6},{5,7},{6,4},{7,5},{8,10},{9,11},{10,... | collective-permute-start | bytes 392 | tf_op jit(solution)/shard_map/ppermute | solution.py:22
  60.5 2.0 %collective-permute-start.7 = (f32[1,32]{1,0:T(1,128)S(1)}, f32[1,32]{1,0:T(1,128)S(1)}, u32[]{:S(2)}, u32[]{:S(2)}) collective-permute-start(f32[1,32]{1,0:T(1,128)S(1)} %get-tuple-element.8), channel_id=1, source_target_pairs={{0,1},{1,0},{2,3},{3,2},{4,5},{5,4},{6,7},{7,6},{8,9},{9,8},{10,11... | collective-permute-start | bytes 392 | tf_op jit(solution)/shard_map/ppermute | solution.py:22
